TPU v7x, 128 devices: a whole 4x4x4 slice. The times are simulated.
128 devices in a mesh: row: 8 (over z, x_hi), col: 16 (over y, x_lo, core).
Axes of the slice: x: 4 (x_hi: 2, x_lo: 2; x = x_hi * 2 + x_lo), y: 4, z: 4, core: 2. Of those that a mesh axis runs over, the one named last changes fastest.
Arguments:
- embed: bfloat16 [32768, 768], P(('row', 'col')), as said below
- cand_tiles: int32 [256], P(('row', 'col')), may hold values from 0 to 7
Outputs:
- counts: float32 [32768], P(('row', 'col'))
- tops: float32 [32768], P(('row', 'col'))
- recount: float32 [256, 256], P(('row', 'col'))
Inputs may be any that keep to these rules, and one draw needn't show every extreme that they name: Rows of embed have norms near 1.
All inputs are finite; a program needn't handle non-finite values.
Results may differ from a plain program's by a relative error of at most 0.0008.
Values may be sent and summed in bfloat16 or wider, within the bound.
A program may use at most 64 MiB of HBM per device.

v0:
```python
import jax
import jax.numpy as jnp
from jax import lax
from jax.sharding import PartitionSpec as P


def largest_divisor(length, bound):
    best = 1
    for candidate in range(1, min(length, bound) + 1):
        if length % candidate == 0:
            best = candidate
    return best


def per_device(embed, cand_tiles):
    tile_len, width = embed.shape
    col_count = lax.axis_size("col")
    row_count = lax.axis_size("row")
    my_row = lax.axis_index("row")
    my_col = lax.axis_index("col")
    col_block = lax.all_gather(embed, "row", axis=0, tiled=True)
    used_tiles = col_count * jnp.arange(row_count, dtype=jnp.int32) + my_col
    col_tile = jnp.repeat(used_tiles, tile_len)
    col_place = jnp.tile(jnp.arange(tile_len, dtype=jnp.int32), row_count)
    used_len = row_count * tile_len

    def weights(row_tile, row_place):
        near = row_tile[:, None]
        far = col_tile[None, :]
        full = near < far
        same = near == far
        itself = jnp.logical_and(same, row_place[:, None] == col_place[None, :])
        row_weight = jnp.logical_or(full, jnp.logical_and(same, jnp.logical_not(itself)))
        return (row_weight, full)

    initial = (
        jnp.zeros((col_count * tile_len,), jnp.float32),
        jnp.full((col_count * tile_len,), -3.0, jnp.float32),
        jnp.zeros((used_len,), jnp.float32),
        jnp.full((used_len,), -3.0, jnp.float32),
    )
    piece = lax.all_gather(embed, "col", axis=0, tiled=True)
    start = jnp.int32(0)
    length = piece.shape[0]
    block = largest_divisor(length, 512)

    def step(number, totals):
        row_sums, row_tops, col_sums, col_tops = totals
        offset = number * block
        rows_here = lax.dynamic_slice_in_dim(piece, offset, block, 0)
        scores = lax.dot_general(
            rows_here, col_block, (((1,), (1,)), ((), ())), preferred_element_type=jnp.float32
        )
        position = start + offset + jnp.arange(block, dtype=jnp.int32)
        row_tile = col_count * my_row + position // tile_len
        row_weight, col_weight = weights(row_tile, position % tile_len)
        expsim = jnp.exp(20.0 * (scores - 1.0))
        row_sums = lax.dynamic_update_slice_in_dim(
            row_sums, jnp.sum(jnp.where(row_weight, expsim, 0.0), axis=1), start + offset, 0
        )
        row_tops = lax.dynamic_update_slice_in_dim(
            row_tops, jnp.max(jnp.where(row_weight, scores, -3.0), axis=1), start + offset, 0
        )
        col_sums = col_sums + jnp.sum(jnp.where(col_weight, expsim, 0.0), axis=0)
        col_tops = jnp.maximum(col_tops, jnp.max(jnp.where(col_weight, scores, -3.0), axis=0))
        return (row_sums, row_tops, col_sums, col_tops)

    row_sums, row_tops, col_sums, col_tops = lax.fori_loop(0, length // block, step, initial)
    col_sums = col_sums.reshape(row_count, tile_len)
    col_tops = col_tops.reshape(row_count, tile_len)
    row_sums = row_sums.reshape(col_count, tile_len)
    row_tops = row_tops.reshape(col_count, tile_len)
    shared_sums, shared_tops = (
        lax.all_to_all(row_sums, "col", split_axis=0, concat_axis=0, tiled=True),
        lax.all_to_all(row_tops, "col", split_axis=0, concat_axis=0, tiled=True),
    )
    mirror_sums, mirror_tops = (
        lax.all_to_all(col_sums, "row", split_axis=0, concat_axis=0, tiled=True),
        lax.all_to_all(col_tops, "row", split_axis=0, concat_axis=0, tiled=True),
    )
    counts = jnp.sum(shared_sums, axis=0) + jnp.sum(mirror_sums, axis=0)
    tops = jnp.maximum(jnp.max(shared_tops, axis=0), jnp.max(mirror_tops, axis=0))
    diagonal_mask = jnp.eye(tile_len, dtype=jnp.bool_)

    def recount_one(tile_number):
        partner = lax.dynamic_slice_in_dim(col_block, tile_number * tile_len, tile_len, 0)
        scores = lax.dot_general(
            embed, partner, (((1,), (1,)), ((), ())), preferred_element_type=jnp.float32
        )
        itself = jnp.logical_and(diagonal_mask, tile_number == my_row)
        return jnp.sum(jnp.where(itself, 0.0, jnp.exp(20.0 * (scores - 1.0))), axis=1)

    recount = lax.map(recount_one, cand_tiles)
    return (counts, tops, recount)


def solution(mesh):
    in_specs = (P(("row", "col"), None), P(("row", "col")))
    out_specs = (P(("row", "col")), P(("row", "col")), P(("row", "col"), None))
    return jax.shard_map(
        per_device, mesh=mesh, in_specs=in_specs, out_specs=out_specs, check_vma=False
    )
```

profile of v0, /device:TPU:1, one launch (start us, length us, event | category | flops | bytes accessed | tf_op | source)
XLA Modules:
  0.0 246.5 jit_solution(5818087782961120045)
XLA Ops:
  7.2 0.7 all-gather.5.cloned.1.call-update
  7.9 0.7 all-gather.3.cloned.1.call-update
  8.7 67.3 %all-gather.5.cloned.1.call-done = bf16[2048,768]{1,0:T(8,128)(2,1)} async-done(((bf16[256,768]{1,0:T(8,128)(2,1)}), bf16[2048,768]{1,0:T(8,128)(2,1)}) %all-gather.5.cloned.1.call-update) | async-done | bytes 3145744 | tf_op jit(solution)/shard_map/all_gather | solution.py:21
  76.0 42.6 %all-gather.3.cloned.1.call-done = bf16[4096,768]{1,0:T(8,128)(2,1)} async-done(((bf16[256,768]{1,0:T(8,128)(2,1)}), bf16[4096,768]{1,0:T(8,128)(2,1)}) %all-gather.3.cloned.1.call-update) | async-done | bytes 6291472 | tf_op jit(solution)/shard_map/all_gather | solution.py:42
  118.5 0.6 broadcast_in_dim.61
  119.1 0.6 broadcast_in_dim.62
  119.7 74.1 %while.36 = (s32[]{:T(128)}, f32[4096]{0:T(1024)}, f32[4096]{0:T(1024)}, f32[2048]{0:T(1024)S(1)}, f32[2048]{0:T(1024)S(1)}, /*index=5*/s32[]{:T(128)}, bf16[409...) while((s32[]{:T(128)}, f32[4096]{0:T(1024)}, ...), condition=%wide.region_5.6_spmd.clone, body=%wide.region_0.5_spmd.clone.sunk | while | flops 1628456448 | bytes 4083949 | solution.py:68
  119.8 0.1 broadcast_bitcast_fusion.2
  119.9 6.3 %fusion.37 = (f32[2048]{0:T(1024)S(1)}, f32[2048]{0:T(1024)S(1)}, f32[512]{0:T(512)S(1)}, f32[512]{0:T(512)S(1)}) fusion(s32[2048]{0:T(1024)S(1)} %bitcast.40, s32[512]{0:T(512)S(1)} %fusion.36, s32[2048]{0:T(1024)S(1)} %bitcast.41, s32[512]{0:T(512)S(1)} %add_select_fusion.3, bf16[2048,768]{1,0:T(8,128)(2,1)} %get-tuple-element.572, ...), kind=kOutput, calls=%fused_computation.19.clone.1 | convolution fusion | flops 1628433408 | bytes 3973124 | tf_op jit(solution)/shard_map/while/body/eval_jaxpr/dot_general | solution.py:51
  126.1 1.4 dynamic_update_slice.35
  127.6 1.4 dynamic_update_slice.34
  129.0 0.1 broadcast_bitcast_fusion.2
  129.1 6.3 %fusion.37 = (f32[2048]{0:T(1024)S(1)}, f32[2048]{0:T(1024)S(1)}, f32[512]{0:T(512)S(1)}, f32[512]{0:T(512)S(1)}) fusion(s32[2048]{0:T(1024)S(1)} %bitcast.40, s32[512]{0:T(512)S(1)} %fusion.36, s32[2048]{0:T(1024)S(1)} %bitcast.41, s32[512]{0:T(512)S(1)} %add_select_fusion.3, bf16[2048,768]{1,0:T(8,128)(2,1)} %get-tuple-element.572, ...), kind=kOutput, calls=%fused_computation.19.clone.1 | convolution fusion | flops 1628433408 | bytes 3973124 | tf_op jit(solution)/shard_map/while/body/eval_jaxpr/dot_general | solution.py:51
  135.4 1.4 dynamic_update_slice.35
  136.9 1.4 dynamic_update_slice.34
  138.4 0.1 broadcast_bitcast_fusion.2
  138.4 6.3 %fusion.37 = (f32[2048]{0:T(1024)S(1)}, f32[2048]{0:T(1024)S(1)}, f32[512]{0:T(512)S(1)}, f32[512]{0:T(512)S(1)}) fusion(s32[2048]{0:T(1024)S(1)} %bitcast.40, s32[512]{0:T(512)S(1)} %fusion.36, s32[2048]{0:T(1024)S(1)} %bitcast.41, s32[512]{0:T(512)S(1)} %add_select_fusion.3, bf16[2048,768]{1,0:T(8,128)(2,1)} %get-tuple-element.572, ...), kind=kOutput, calls=%fused_computation.19.clone.1 | convolution fusion | flops 1628433408 | bytes 3973124 | tf_op jit(solution)/shard_map/while/body/eval_jaxpr/dot_general | solution.py:51
  144.7 1.4 dynamic_update_slice.35
  146.2 1.4 dynamic_update_slice.34
  147.6 0.1 broadcast_bitcast_fusion.2
  147.7 6.3 %fusion.37 = (f32[2048]{0:T(1024)S(1)}, f32[2048]{0:T(1024)S(1)}, f32[512]{0:T(512)S(1)}, f32[512]{0:T(512)S(1)}) fusion(s32[2048]{0:T(1024)S(1)} %bitcast.40, s32[512]{0:T(512)S(1)} %fusion.36, s32[2048]{0:T(1024)S(1)} %bitcast.41, s32[512]{0:T(512)S(1)} %add_select_fusion.3, bf16[2048,768]{1,0:T(8,128)(2,1)} %get-tuple-element.572, ...), kind=kOutput, calls=%fused_computation.19.clone.1 | convolution fusion | flops 1628433408 | bytes 3973124 | tf_op jit(solution)/shard_map/while/body/eval_jaxpr/dot_general | solution.py:51
  154.0 1.4 dynamic_update_slice.35
  155.5 1.4 dynamic_update_slice.34
  156.9 0.1 broadcast_bitcast_fusion.2
  157.0 6.3 %fusion.37 = (f32[2048]{0:T(1024)S(1)}, f32[2048]{0:T(1024)S(1)}, f32[512]{0:T(512)S(1)}, f32[512]{0:T(512)S(1)}) fusion(s32[2048]{0:T(1024)S(1)} %bitcast.40, s32[512]{0:T(512)S(1)} %fusion.36, s32[2048]{0:T(1024)S(1)} %bitcast.41, s32[512]{0:T(512)S(1)} %add_select_fusion.3, bf16[2048,768]{1,0:T(8,128)(2,1)} %get-tuple-element.572, ...), kind=kOutput, calls=%fused_computation.19.clone.1 | convolution fusion | flops 1628433408 | bytes 3973124 | tf_op jit(solution)/shard_map/while/body/eval_jaxpr/dot_general | solution.py:51
  163.4 1.5 dynamic_update_slice.35
  164.8 1.4 dynamic_update_slice.34
  166.4 6.3 %fusion.37 = (f32[2048]{0:T(1024)S(1)}, f32[2048]{0:T(1024)S(1)}, f32[512]{0:T(512)S(1)}, f32[512]{0:T(512)S(1)}) fusion(s32[2048]{0:T(1024)S(1)} %bitcast.40, s32[512]{0:T(512)S(1)} %fusion.36, s32[2048]{0:T(1024)S(1)} %bitcast.41, s32[512]{0:T(512)S(1)} %add_select_fusion.3, bf16[2048,768]{1,0:T(8,128)(2,1)} %get-tuple-element.572, ...), kind=kOutput, calls=%fused_computation.19.clone.1 | convolution fusion | flops 1628433408 | bytes 3973124 | tf_op jit(solution)/shard_map/while/body/eval_jaxpr/dot_general | solution.py:51
  172.7 1.5 dynamic_update_slice.35
  174.1 1.4 dynamic_update_slice.34
  175.7 6.3 %fusion.37 = (f32[2048]{0:T(1024)S(1)}, f32[2048]{0:T(1024)S(1)}, f32[512]{0:T(512)S(1)}, f32[512]{0:T(512)S(1)}) fusion(s32[2048]{0:T(1024)S(1)} %bitcast.40, s32[512]{0:T(512)S(1)} %fusion.36, s32[2048]{0:T(1024)S(1)} %bitcast.41, s32[512]{0:T(512)S(1)} %add_select_fusion.3, bf16[2048,768]{1,0:T(8,128)(2,1)} %get-tuple-element.572, ...), kind=kOutput, calls=%fused_computation.19.clone.1 | convolution fusion | flops 1628433408 | bytes 3973124 | tf_op jit(solution)/shard_map/while/body/eval_jaxpr/dot_general | solution.py:51
  181.9 1.4 dynamic_update_slice.35
  183.3 1.3 dynamic_update_slice.34
  184.8 6.3 %fusion.37 = (f32[2048]{0:T(1024)S(1)}, f32[2048]{0:T(1024)S(1)}, f32[512]{0:T(512)S(1)}, f32[512]{0:T(512)S(1)}) fusion(s32[2048]{0:T(1024)S(1)} %bitcast.40, s32[512]{0:T(512)S(1)} %fusion.36, s32[2048]{0:T(1024)S(1)} %bitcast.41, s32[512]{0:T(512)S(1)} %add_select_fusion.3, bf16[2048,768]{1,0:T(8,128)(2,1)} %get-tuple-element.572, ...), kind=kOutput, calls=%fused_computation.19.clone.1 | convolution fusion | flops 1628433408 | bytes 3973124 | tf_op jit(solution)/shard_map/while/body/eval_jaxpr/dot_general | solution.py:51
  191.1 1.4 dynamic_update_slice.35
  192.5 1.3 dynamic_update_slice.34
  193.8 12.9 %all_to_all.36 = f32[8,1,256]{2,1,0:T(1,128)S(1)} all-to-all(f32[8,1,256]{2,1,0:T(1,128)S(1)} %bitcast.39), channel_id=1, replica_groups=mesh['row'=8,'col'=16] {'row'}, dimensions={0} | all-to-all | bytes 16384 | tf_op jit(solution)/shard_map/all_to_all | solution.py:79
  206.7 8.9 %all_to_all.37 = f32[8,1,256]{2,1,0:T(1,128)S(1)} all-to-all(f32[8,1,256]{2,1,0:T(1,128)S(1)} %bitcast.38), channel_id=1, replica_groups=mesh['row'=8,'col'=16] {'row'}, dimensions={0} | all-to-all | bytes 16384 | tf_op jit(solution)/shard_map/all_to_all | solution.py:78
  215.6 6.9 %all-to-all-start.2 = ((f32[16,1,256]{2,1,0:T(1,128)}), f32[16,1,256]{2,1,0:T(1,128)S(1)}, u32[]{:S(2)}, u32[]{:S(2)}) async-start(f32[16,1,256]{2,1,0:T(1,128)} %bitcast.2), calls=%async_computation.2 | async-start | bytes 32768 | tf_op jit(solution)/shard_map/all_to_all | solution.py:75
  222.4 5.6 %all-to-all-done.2 = f32[16,1,256]{2,1,0:T(1,128)S(1)} async-done(((f32[16,1,256]{2,1,0:T(1,128)}), f32[16,1,256]{2,1,0:T(1,128)S(1)}, u32[]{:S(2)}, u32[]{:S(2)}) %all-to-all-start.2) | async-done | bytes 16416 | tf_op jit(solution)/shard_map/all_to_all | solution.py:75
  228.1 3.7 %all-to-all-start = ((f32[16,1,256]{2,1,0:T(1,128)}), f32[16,1,256]{2,1,0:T(1,128)S(1)}, u32[]{:S(2)}, u32[]{:S(2)}) async-start(f32[16,1,256]{2,1,0:T(1,128)} %bitcast), calls=%async_computation | async-start | bytes 32768 | tf_op jit(solution)/shard_map/all_to_all | solution.py:74
  231.7 6.6 %while.35 = (s32[]{:T(128)}, f32[2,256]{1,0:T(2,128)S(1)}, s32[2]{0:T(128)S(1)}, s32[]{:T(128)}, bf16[2048,768]{1,0:T(8,128)(2,1)}, /*index=5*/bf16[256,768]{1,0...) while((s32[]{:T(128)}, f32[2,256]{1,0:T(2,128)S(1)}, s32[2]{0:T(128)S(1)}, ...), condition=%wide.region_12.13_spmd.clone, body=%wide.region_10.12_spmd.clone.sunk | while | flops 101056264 | bytes 789681 | solution.py:93
  231.8 0.6 dynamic_slice.36
  233.7 1.4 fusion.34
  235.1 0.6 dynamic_slice.36
  236.9 1.4 fusion.34
  238.4 0.6 max.13
  239.1 0.6 add.149
  (70 shorter events, 0.9 us)
Async XLA Ops:
  7.2 68.8 %all-gather.5.cloned.1.call-start = ((), (), s32[]{:S(2)}) async-start(), calls=%async_computation.5 | async-start | bytes 3538944 | tf_op jit(solution)/shard_map/all_gather | solution.py:21
  7.9 110.6 %all-gather.3.cloned.1.call-start = ((), (), s32[]{:S(2)}) async-start(), calls=%async_computation.4 | async-start | bytes 6684672 | tf_op jit(solution)/shard_map/all_gather | solution.py:42
  119.7 112.0 %copy-start = (bf16[256,768]{1,0:T(8,128)(2,1)S(1)}, bf16[256,768]{1,0:T(8,128)(2,1)}, u32[]{:S(2)}) copy-start(bf16[256,768]{1,0:T(8,128)(2,1)} %param.6) | copy-start | bytes 1179652
  119.7 112.0 %copy-start.2 = (s32[2]{0:T(128)S(1)}, s32[2]{0:T(128)}, u32[]{:S(2)}) copy-start(s32[2]{0:T(128)} %param.7) | copy-start | bytes 28
  215.6 12.5 %all-to-all-start.2 = ((f32[16,1,256]{2,1,0:T(1,128)}), f32[16,1,256]{2,1,0:T(1,128)S(1)}, u32[]{:S(2)}, u32[]{:S(2)}) async-start(f32[16,1,256]{2,1,0:T(1,128)} %bitcast.2), calls=%async_computation.2 | async-start | bytes 32768 | tf_op jit(solution)/shard_map/all_to_all | solution.py:75
  228.1 11.0 %all-to-all-start = ((f32[16,1,256]{2,1,0:T(1,128)}), f32[16,1,256]{2,1,0:T(1,128)S(1)}, u32[]{:S(2)}, u32[]{:S(2)}) async-start(f32[16,1,256]{2,1,0:T(1,128)} %bitcast), calls=%async_computation | async-start | bytes 32768 | tf_op jit(solution)/shard_map/all_to_all | solution.py:74
  238.3 1.3 copy-start.1
Sparse Core Ops, SparseCore 0:
  10.3 65.6 all-gather.4
  77.7 40.8 all-gather.2
where the time goes:
time: 247 us; the launch traced here: 246 us
  waiting for transfers between devices  117 us (47%)
  matrix products  53 us (21%)
  local copies, waits for them, and re-layouts  25.9 us (10%)
  blocking collectives  21.7 us (9%)
  between operations  14.1 us (6%)
  starting transfers between devices  10.6 us (4%)
  loops' own time  2.77 us (1%)
    all_gather x1, waiting for transfers between devices, per_device(): col_block = lax.all_gather(embed, 'row', axis=0, tiled=True)  67.3 us
    dot_general x8, matrix products, step(): lax.dot_general(rows_here, col_block, (((1,), (1,)), ((), ())), preferred...  50.3 us
    all_gather x1, waiting for transfers between devices, per_device(): piece = lax.all_gather(embed, 'col', axis=0, tiled=True)  42.6 us
    all_to_all x1, blocking collectives, per_device(): lax.all_to_all(col_tops, 'row', split_axis=0, concat_axis=0, tiled=True)  12.9 us
    dynamic_update_slice x8, local copies, waits for them, and re-layouts, step(): lax.dynamic_update_slice_in_dim(row_tops, jnp.max(jnp.where(row_weight, s...  11.4 us
    dynamic_update_slice x8, local copies, waits for them, and re-layouts, step(): lax.dynamic_update_slice_in_dim(row_sums, jnp.sum(jnp.where(row_weight, e...  11.3 us
    all_to_all x1, blocking collectives, per_device(): lax.all_to_all(col_sums, 'row', split_axis=0, concat_axis=0, tiled=True)  8.89 us
    all_to_all x1, starting transfers between devices, per_device(): lax.all_to_all(row_tops, 'col', split_axis=0, concat_axis=0, tiled=True)  6.86 us
  transfers between devices with their start and end apart: 4, of which 3 were waited for; matrix products, arithmetic and copies ran while one was open for 2% of the time, Pallas kernels for 0%

commit v1 on v0

v1 whole, which is shorter than its diff:
```python
import jax
import jax.numpy as jnp
from jax import lax
from jax.experimental import pallas as pl
from jax.experimental.pallas import tpu as pltpu
from jax.sharding import PartitionSpec as P

MESH = pl.DeviceIdType.MESH
ROWS = 256
WIDTH = 768
SCALE = 20.0 * 1.4426950408889634
LOWEST = -3.0
TRANSPOSED = (((1,), (1,)), ((), ()))
DIRECTIONS = ((1, 0, 0), (3, 0, 0), (0, 1, 0), (0, 3, 0), (0, 0, 1), (0, 0, 3))
CHUNKS = 4
TILES = (
   (0, 0, 0),
   (0, 0, 1),
   (0, 0, 2),
   (0, 0, 3),
   (0, 1, 0),
   (0, 2, 0),
   (1, 0, 2),
   (1, 0, 3),
   (2, 2, 0),
   (2, 3, 0),
   (3, 0, 0),
   (3, 3, 0),
)
ROUTES = (
    (),
   (4, 4, 4, 4),
   (4, 5, 4, 4),
   (5, 5, 5, 5),
   (2, 2, 2, 2),
   (2, 2, 2, 2),
   (0, 0, 5, 5),
   (0, 0, 0, 0),
   (3, 3, 3, 3),
   (1, 1, 1, 1),
   (1, 1, 1, 1),
   (3, 3, 3, 3),
)
PAIRS = (
   (4, 0, 0),
   (1, 0, 0),
   (10, 0, 0),
   (1, 3, 1),
   (3, 4, 0),
   (1, 4, 0),
   (1, 10, 0),
   (3, 10, 0),
   (4, 10, 0),
   (11, 4, 0),
   (7, 10, 0),
   (7, 4, 0),
   (11, 3, 0),
   (11, 1, 0),
   (7, 1, 0),
   (7, 11, 0),
   (2, 11, 0),
   (2, 4, 0),
   (6, 11, 0),
   (6, 10, 1),
   (6, 4, 0),
   (5, 0, 1),
   (9, 4, 1),
   (9, 1, 0),
   (9, 0, 0),
   (9, 7, 0),
   (5, 11, 0),
   (5, 7, 0),
   (5, 1, 0),
   (5, 2, 1),
   (5, 6, 0),
   (8, 5, 1),
   (8, 7, 0),
   (8, 1, 0),
   (8, 2, 1),
)
ARRIVALS = (
    ((1, 0), (3, 0), (4, 0), (10, 0), (1, 1), (3, 1), (4, 1), (10, 1), (7, 0), (11, 0), (1, 2), (3, 2), (4, 2), (10, 2), (7, 1), (11, 1), (1, 3), (3, 3), (4, 3), (10, 3),),
    ((7, 2), (11, 2),),
    (),
    ((2, 0), (2, 1), (5, 0), (9, 0),),
    ((7, 3), (11, 3),),
    (),
    ((2, 2), (5, 1), (9, 1), (6, 2),),
    (),
    ((6, 0), (8, 0), (2, 3), (5, 2), (9, 2), (6, 3),),
    ((6, 1), (8, 1),),
    ((5, 3), (9, 3),),
    (),
    ((8, 2),),
    (),
    (),
    ((8, 3),),
    (),
    (),
)
COUNT = len(TILES)
PIECE = ROWS // CHUNKS


def minus(a, b):
    return tuple((p - q) % 4 for p, q in zip(a, b))


def parent(tile, chunk):
    return TILES.index(minus(TILES[tile], DIRECTIONS[ROUTES[tile][chunk]]))


def children():
    table = {}
    for tile in range(1, COUNT):
        for chunk in range(CHUNKS):
            table.setdefault((parent(tile, chunk), chunk), []).append((tile, chunk))
    return table


CHILDREN = children()
ROW_TILES = sorted({x for x, _, _ in PAIRS})
SHARED_TILES = sorted({y for _, y, _ in PAIRS} | {0})
COL_TILES = sorted({y for _, y, one in PAIRS if not one})


def kept_rows():
    kept = []
    fill = [2] * COUNT
    for number, (x, y, one) in enumerate(PAIRS):
        apart = minus(TILES[y], TILES[x])
        if apart[1] == 0 and apart[0] % 2 == 0:
            back = minus(TILES[x], TILES[y])
            left = (x, fill[x], apart[2] * 2 + apart[0] // 2)
            fill[x] += 1
            right = None
            if not one:
                right = (y, fill[y], back[2] * 2 + back[0] // 2)
                fill[y] += 1
            kept.append((number, left, right))
    return kept


KEPT = kept_rows()
KEPT_OF = {number: place for place, (number, _, _) in enumerate(KEPT)}
SPARE_ROW = COUNT
SPARE_KEPT = len(KEPT)
SPARE_COL = COUNT
KEPT_COL = COUNT + 1


def slots(number):
    x, y, one = PAIRS[number]
    kept = KEPT_OF.get(number, SPARE_KEPT)
    if one:
        col = SPARE_COL
    elif kept != SPARE_KEPT:
        col = KEPT_COL + kept
    else:
        col = y
    return (x, y, x, kept, col)


NOTHING = (0, 0, SPARE_ROW, SPARE_KEPT, SPARE_COL)
ROUNDS = (len(PAIRS) + 1) // 2


def first_use(tile):
    for number, (_, y, _) in enumerate(PAIRS):
        if y == tile:
            return number // 2
    return None


def kernel(
    cand_ref, embed_ref, counts_ref, tops_ref, recount_ref,
    tiles, near, far, row_sums, row_tops, kept_sums, col_sums, col_tops,
    outbox, inbox, table,
    own_sem, hop_send, hop_recv, twin_send, twin_recv, post_send, post_recv,
):
    my_row = lax.axis_index("row")
    my_col = lax.axis_index("col")
    z, x_hi = my_row // 2, my_row % 2
    y, x_lo, core = my_col // 4, (my_col // 2) % 2, my_col % 2
    x = x_hi * 2 + x_lo
    other = 1 - core

    def device(offset, at_core):
        px = (x + offset[0]) % 4
        py = (y + offset[1]) % 4
        pz = (z + offset[2]) % 4
        return (pz * 2 + px // 2, py * 4 + (px % 2) * 2 + at_core)

    def span(chunk):
        return pl.ds(chunk * PIECE, PIECE)

    def hop(tile, chunk):
        origin = parent(tile, chunk)
        step = DIRECTIONS[ROUTES[tile][chunk]]
        source = embed_ref.at[span(chunk)] if origin == 0 else tiles.at[origin, core, span(chunk)]
        return pltpu.make_async_remote_copy(
            src_ref=source,
            dst_ref=tiles.at[tile, core, span(chunk)],
            send_sem=hop_send.at[tile, chunk],
            recv_sem=hop_recv.at[tile, chunk],
            device_id=device(minus((0, 0, 0), step), core),
            device_id_type=MESH,
        )

    def twin(tile, chunk):
        source = embed_ref.at[span(chunk)] if tile == 0 else tiles.at[tile, core, span(chunk)]
        return pltpu.make_async_remote_copy(
            src_ref=source,
            dst_ref=tiles.at[tile, core, span(chunk)],
            send_sem=twin_send.at[tile],
            recv_sem=twin_recv.at[tile],
            device_id=device((0, 0, 0), other),
            device_id_type=MESH,
        )

    def twin_whole(tile):
        return pltpu.make_async_remote_copy(
            src_ref=tiles.at[tile, other],
            dst_ref=tiles.at[tile, other],
            send_sem=twin_send.at[tile],
            recv_sem=twin_recv.at[tile],
            device_id=device((0, 0, 0), other),
            device_id_type=MESH,
        )

    def post(tile, at_core):
        return pltpu.make_async_remote_copy(
            src_ref=outbox.at[tile, at_core],
            dst_ref=inbox.at[tile, core],
            send_sem=post_send.at[tile, at_core],
            recv_sem=post_recv.at[tile, core],
            device_id=device(TILES[tile], at_core),
            device_id_type=MESH,
        )

    def posted(tile, from_core):
        return pltpu.make_async_remote_copy(
            src_ref=outbox.at[tile, from_core],
            dst_ref=inbox.at[tile, from_core],
            send_sem=post_send.at[tile, from_core],
            recv_sem=post_recv.at[tile, from_core],
            device_id=device(TILES[tile], from_core),
            device_id_type=MESH,
        )

    own = pltpu.make_async_copy(embed_ref, tiles.at[0, core], own_sem)
    own.start()

    barrier = pltpu.get_barrier_semaphore()
    for step in DIRECTIONS:
        pl.semaphore_signal(barrier, inc=1, device_id=device(step, core), device_id_type=MESH)
    pl.semaphore_signal(barrier, inc=1, device_id=device((0, 0, 0), other), device_id_type=MESH)
    pl.semaphore_wait(barrier, 7)

    for chunk in range(CHUNKS):
        for tile, piece in CHILDREN.get((0, chunk), ()):
            hop(tile, piece).start()
    for chunk in range(CHUNKS):
        twin(0, chunk).start()

    row_sums[...] = jnp.zeros_like(row_sums)
    col_sums[...] = jnp.zeros_like(col_sums)
    row_tops[...] = jnp.full_like(row_tops, LOWEST)
    col_tops[...] = jnp.full_like(col_tops, LOWEST)
    far[...] = jnp.zeros_like(far)

    def multiply(target, left, right):
        target[...] = lax.dot_general(
            tiles[left, core], tiles[right].reshape(2 * ROWS, WIDTH), TRANSPOSED,
            preferred_element_type=jnp.float32,
        )

    def halves(op, values):
        return (
            op(values[:, 0:128], values[:, 128:256]),
            op(values[:, 256:384], values[:, 384:512]),
        )

    def reduce(source, row, kept, col, own_pair=False):
        sums = tops = None
        for first in range(0, ROWS, 64):
            part = pl.ds(first, 64)
            scores = source[part, :]
            weights = jnp.exp2(scores * SCALE - SCALE)
            if own_pair:
                place = lax.broadcasted_iota(jnp.int32, (64, 2 * ROWS), 0) + (first + core * ROWS)
                itself = place == lax.broadcasted_iota(jnp.int32, (64, 2 * ROWS), 1)
                weights = jnp.where(itself, 0.0, weights)
                scores = jnp.where(itself, LOWEST, scores)
            left, right = halves(jnp.add, weights)
            row_sums[row, part] += left + right
            kept_sums[kept, part] = jnp.where(core == 0, left, right)
            row_tops[row, part] = jnp.maximum(
                row_tops[row, part], jnp.maximum(*halves(jnp.maximum, scores))
            )
            if own_pair:
                continue
            for at in range(0, 64, 8):
                sums = weights[at:at + 8] if sums is None else sums + weights[at:at + 8]
                high = scores[at:at + 8]
                tops = high if tops is None else jnp.maximum(tops, high)
        if not own_pair:
            col_sums[col] += sums
            col_tops[col] = jnp.maximum(col_tops[col], tops)

    def arrive(tile, chunk):
        hop(tile, chunk).wait_recv()
        for child, piece in CHILDREN.get((tile, chunk), ()):
            hop(child, piece).start()
        if tile in SHARED_TILES:
            twin(tile, chunk).start()

    own.wait()
    twin_whole(0).wait_recv()
    multiply(near, 0, 0)
    reduce(near, 0, SPARE_KEPT + 1, SPARE_COL, own_pair=True)

    def arrivals(number):
        def run():
            for tile, chunk in ARRIVALS[number]:
                arrive(tile, chunk)
            for tile in SHARED_TILES:
                if tile != 0 and first_use(tile) == number:
                    twin_whole(tile).wait_recv()
            values = []
            for step in (2 * number, 2 * number + 1):
                values += slots(step) if step < len(PAIRS) else NOTHING
            return tuple(jnp.int32(v) for v in values)
        return run

    def round_of(number, before):
        now = lax.switch(number, [arrivals(n) for n in range(ROUNDS)])
        multiply(near, now[0], now[1])
        reduce(far, *before)
        multiply(far, now[5], now[6])
        reduce(near, *now[2:5])
        return tuple(now[7:10])

    last = lax.fori_loop(
        0, ROUNDS, round_of, tuple(jnp.int32(v) for v in NOTHING[2:5])
    )
    reduce(far, *last)

    def across(values, op):
        return op(values.T, axis=0, keepdims=True)

    sends = []
    for tile in list(range(1, COUNT)) + [0]:
        for at_core in (0, 1):
            lanes = pl.ds(at_core * ROWS, ROWS)
            sums = jnp.zeros((1, ROWS), jnp.float32)
            tops = jnp.full((1, ROWS), LOWEST, jnp.float32)
            if tile in COL_TILES:
                sums = jnp.sum(col_sums[tile, :, lanes], axis=0, keepdims=True)
                tops = jnp.max(col_tops[tile, :, lanes], axis=0, keepdims=True)
            for place, (_, _, right) in enumerate(KEPT):
                if right is not None and right[0] == tile:
                    extra = jnp.sum(col_sums[KEPT_COL + place, :, lanes], axis=0, keepdims=True)
                    sums = sums + extra
                    outbox[tile, at_core, pl.ds(right[1], 1), :] = extra
                    tops = jnp.maximum(
                        tops, jnp.max(col_tops[KEPT_COL + place, :, lanes], axis=0, keepdims=True)
                    )
            outbox[tile, at_core, 0:1, :] = sums
            outbox[tile, at_core, 1:2, :] = tops
        if tile in ROW_TILES or tile == 0:
            outbox[tile, core, 0:1, :] += across(row_sums[tile], jnp.sum)
            outbox[tile, core, 1:2, :] = jnp.maximum(
                outbox[tile, core, 1:2, :], across(row_tops[tile], jnp.max)
            )
        for place, (_, left, _) in enumerate(KEPT):
            if left[0] == tile:
                outbox[tile, core, pl.ds(left[1], 1), :] = across(kept_sums[place], jnp.sum)
        if tile != 0:
            post(tile, core).start()
        if tile in COL_TILES:
            post(tile, other).start()
    table[0:1, :] = across(kept_sums[SPARE_KEPT + 1], jnp.sum)

    sums = outbox[0, core, 0:1, :]
    tops = outbox[0, core, 1:2, :]
    for tile in list(range(1, COUNT)) + [0]:
        for from_core in (core, other):
            if from_core is core and tile == 0:
                continue
            if from_core is other and tile not in COL_TILES:
                continue
            posted(tile, from_core).wait_recv()
            sums = sums + inbox[tile, from_core, 0:1, :]
            tops = jnp.maximum(tops, inbox[tile, from_core, 1:2, :])
    counts_ref[...] = sums
    tops_ref[...] = tops
    for _, left, right in KEPT:
        for side in (left, right):
            if side is not None:
                where = outbox if side[0] == 0 else inbox
                table[pl.ds(side[2], 1), :] = where[side[0], core, pl.ds(side[1], 1), :]
    for number in range(2):
        chosen = cand_ref[number]
        apart = ((chosen // 2 - z + 4) % 4) * 2 + (chosen % 2 - x_hi + 2) % 2
        recount_ref[pl.ds(number, 1), :] = table[pl.ds(apart, 1), :]

    for tile in range(1, COUNT):
        for chunk in range(CHUNKS):
            hop(tile, chunk).wait_send()
    for tile in SHARED_TILES:
        twin_whole(tile).wait_send()
    for tile in range(COUNT):
        if tile != 0:
            post(tile, core).wait_send()
        if tile in COL_TILES:
            post(tile, other).wait_send()


def per_device(embed, cand_tiles):
    vector = pltpu.VMEM
    semaphores = pltpu.SemaphoreType.DMA
    counts, tops, recount = pl.pallas_call(
        kernel,
        out_shape=(
            jax.ShapeDtypeStruct((1, ROWS), jnp.float32),
            jax.ShapeDtypeStruct((1, ROWS), jnp.float32),
            jax.ShapeDtypeStruct((2, ROWS), jnp.float32),
        ),
        in_specs=[
            pl.BlockSpec(memory_space=pltpu.SMEM),
            pl.BlockSpec(memory_space=pl.ANY),
        ],
        out_specs=[pl.BlockSpec(memory_space=pltpu.VMEM)] * 3,
        scratch_shapes=[
            vector((COUNT, 2, ROWS, WIDTH), jnp.bfloat16),
            vector((ROWS, 2 * ROWS), jnp.float32),
            vector((ROWS, 2 * ROWS), jnp.float32),
            vector((COUNT + 1, ROWS, 128), jnp.float32),
            vector((COUNT + 1, ROWS, 128), jnp.float32),
            vector((SPARE_KEPT + 2, ROWS, 128), jnp.float32),
            vector((KEPT_COL + len(KEPT), 8, 2 * ROWS), jnp.float32),
            vector((KEPT_COL + len(KEPT), 8, 2 * ROWS), jnp.float32),
            vector((COUNT, 2, 8, ROWS), jnp.float32),
            vector((COUNT, 2, 8, ROWS), jnp.float32),
            vector((8, ROWS), jnp.float32),
            semaphores,
            semaphores((COUNT, CHUNKS)),
            semaphores((COUNT, CHUNKS)),
            semaphores((COUNT,)),
            semaphores((COUNT,)),
            semaphores((COUNT, 2)),
            semaphores((COUNT, 2)),
        ],
        compiler_params=pltpu.CompilerParams(
            collective_id=0, has_side_effects=True, vmem_limit_bytes=56 * 1024 * 1024
        ),
        cost_estimate=pl.CostEstimate(
            flops=37 * 2 * ROWS * 2 * ROWS * WIDTH,
            bytes_accessed=COUNT * 2 * ROWS * WIDTH * 2,
            transcendentals=37 * ROWS * 2 * ROWS,
        ),
    )(cand_tiles, embed)
    return counts.reshape(ROWS), tops.reshape(ROWS), recount


def solution(mesh):
    in_specs = (P(("row", "col"), None), P(("row", "col")))
    out_specs = (P(("row", "col")), P(("row", "col")), P(("row", "col"), None))
    return jax.shard_map(
        per_device, mesh=mesh, in_specs=in_specs, out_specs=out_specs, check_vma=False
    )
```

time: 247 us -> 50.6 us (0.20)
  waiting for transfers between devices: 117 us -> 0 us
  matrix products: 53 us -> 0 us
  Pallas kernels: 0 us -> 47.5 us
  local copies, waits for them, and re-layouts: 25.9 us -> 2.33 us
  blocking collectives: 21.7 us -> 0 us
  between operations: 14.1 us -> 0.66 us
  starting transfers between devices: 10.6 us -> 0 us
  loops' own time: 2.77 us -> 0 us
    all_gather x2 -> x0, waiting for transfers between devices: 110 us -> none  [the longest x1 67.3 us: per_device(): col_block = lax.all_gather(embed, 'row', axis=0, tiled=True)]
    dot_general x10 -> x0, matrix products: 53 us -> none  [the longest x8 50.3 us: step(): lax.dot_general(rows_here, col_block, (((1,), (1,)), ((), ())), preferred...]
    pallas_call x0 -> x1, Pallas kernels: none -> 47.5 us  [per_device(): pl.pallas_call(kernel, out_shape=(jax.ShapeDtypeStruct((1, ROWS), jnp.flo...]
    dynamic_update_slice x18 -> x0, local copies, waits for them, and re-layouts: 22.8 us -> none  [the longest x8 11.4 us: step(): lax.dynamic_update_slice_in_dim(row_tops, jnp.max(jnp.where(row_weight, s...]
    all_to_all x2 -> x0, blocking collectives: 21.7 us -> none  [the longest x1 12.9 us: per_device(): lax.all_to_all(col_tops, 'row', split_axis=0, concat_axis=0, tiled=True)]
    all_to_all x2 -> x0, starting transfers between devices: 10.5 us -> none  [the longest x1 6.86 us: per_device(): lax.all_to_all(row_tops, 'col', split_axis=0, concat_axis=0, tiled=True)]
    all_to_all x2 -> x0, waiting for transfers between devices: 5.63 us -> none  [the longest x1 5.63 us: per_device(): lax.all_to_all(row_tops, 'col', split_axis=0, concat_axis=0, tiled=True)]
    another operation x2 -> x0, loops' own time: 2.77 us -> none  [the longest x1 2.63 us: per_device(): recount = lax.map(recount_one, cand_tiles)]
  transfers between devices with their start and end apart: 4 -> 0, of which waited for: 3 -> 0; matrix products, arithmetic and copies ran while one was open for 2% -> 0% of each run, Pallas kernels for 0% -> 0%
where the time goes in v1:
time: 50.6 us; the launch traced here: 50.5 us
  Pallas kernels  47.5 us (94%)
  local copies, waits for them, and re-layouts  2.33 us (5%)
  between operations  0.66 us (1%)
    pallas_call x1, Pallas kernels, per_device(): pl.pallas_call(kernel, out_shape=(jax.ShapeDtypeStruct((1, ROWS), jnp.flo...  47.5 us
    unnamed x9, local copies, waits for them, and re-layouts  2.33 us

profile of v1, /device:TPU:1, one launch (start us, length us, event | category | flops | bytes accessed | tf_op | source)
XLA Modules:
  0.0 50.5 jit_solution(8723905270120375686)
XLA Ops:
  0.6 47.5 %shard_map.49 = (f32[1,256]{1,0:T(1,128)}, f32[1,256]{1,0:T(1,128)}, f32[2,256]{1,0:T(2,128)}) custom-call(s32[2]{0:T(128)} %cand_ref.1, bf16[256,768]{1,0:T(8,128)(2,1)} %embed_ref.1), custom_call_target="tpu_custom_call" | custom-call | flops 7449083904 | bytes 9437184 | tf_op jit(solution)/shard_map/pallas_call | solution.py:423
  48.1 0.0 copy-start.2
  48.1 0.0 copy-start.1
  48.1 0.6 %copy-done.2 = f32[1,256]{1,0:T(1,128)S(1)} copy-done((f32[1,256]{1,0:T(1,128)S(1)}, f32[1,256]{1,0:T(1,128)}, u32[]{:S(2)}) %copy-start.2) | copy-done | bytes 1048
  48.8 0.0 copy-start
  48.8 0.6 %copy.8 = f32[256]{0:T(256)} copy(f32[256]{0:T(256)S(1)} %bitcast.3) | data formatting | bytes 2048
  49.3 0.0 copy-done.1
  49.3 0.6 %copy.9 = f32[256]{0:T(256)} copy(f32[256]{0:T(256)S(1)} %bitcast.2) | data formatting | bytes 2048
  49.9 0.0 copy-done
  49.9 0.6 %copy.10 = f32[2,256]{1,0:T(2,128)} copy(f32[2,256]{1,0:T(2,128)S(1)} %copy-done) | data formatting | bytes 4096
Async XLA Ops:
  48.1 0.6 %copy-start.2 = (f32[1,256]{1,0:T(1,128)S(1)}, f32[1,256]{1,0:T(1,128)}, u32[]{:S(2)}) copy-start(f32[1,256]{1,0:T(1,128)} %get-tuple-element.6) | copy-start | bytes 3076
  48.1 1.2 %copy-start.1 = (f32[1,256]{1,0:T(1,128)S(1)}, f32[1,256]{1,0:T(1,128)}, u32[]{:S(2)}) copy-start(f32[1,256]{1,0:T(1,128)} %get-tuple-element.7) | copy-start | bytes 3076
  48.8 1.1 %copy-start = (f32[2,256]{1,0:T(2,128)S(1)}, f32[2,256]{1,0:T(2,128)}, u32[]{:S(2)}) copy-start(f32[2,256]{1,0:T(2,128)} %get-tuple-element.14) | copy-start | bytes 6148

commit v2 on v1

--- a/solution.py
+++ b/solution.py
@@ -15,86 +15,87 @@
 CHUNKS = 4
 TILES = (
    (0, 0, 0),
-   (0, 0, 1),
-   (0, 0, 2),
    (0, 0, 3),
-   (0, 1, 0),
+   (0, 1, 2),
+   (0, 1, 3),
    (0, 2, 0),
-   (1, 0, 2),
-   (1, 0, 3),
-   (2, 2, 0),
-   (2, 3, 0),
+   (0, 2, 2),
+   (0, 3, 0),
+   (1, 0, 0),
+   (2, 0, 0),
+   (2, 0, 1),
    (3, 0, 0),
-   (3, 3, 0),
+   (3, 0, 1),
 )
 ROUTES = (
     (),
-   (4, 4, 4, 4),
-   (4, 5, 4, 4),
+   (5, 5, 5, 5),
    (5, 5, 5, 5),
    (2, 2, 2, 2),
+   (3, 3, 3, 3),
    (2, 2, 2, 2),
-   (0, 0, 5, 5),
+   (3, 3, 3, 3),
    (0, 0, 0, 0),
-   (3, 3, 3, 3),
+   (0, 0, 5, 0),
+   (1, 1, 1, 4),
    (1, 1, 1, 1),
-   (1, 1, 1, 1),
-   (3, 3, 3, 3),
+   (4, 4, 4, 4),
 )
+FIRST = ((1, 2), (6, 2), (7, 2), (10, 0), (1, 3), (6, 3), (7, 3), (10, 1), (1, 0), (6, 0), (7, 0), (10, 2), (1, 1), (6, 1), (7, 1), (10, 3),)
 PAIRS = (
-   (4, 0, 0),
    (1, 0, 0),
-   (10, 0, 0),
-   (1, 3, 1),
-   (3, 4, 0),
-   (1, 4, 0),
+   (6, 0, 0),
+   (7, 0, 0),
+   (7, 10, 1),
+   (1, 6, 0),
+   (6, 10, 0),
+   (1, 7, 0),
+   (6, 7, 0),
    (1, 10, 0),
    (3, 10, 0),
-   (4, 10, 0),
-   (11, 4, 0),
-   (7, 10, 0),
-   (7, 4, 0),
-   (11, 3, 0),
+   (11, 7, 0),
+   (11, 6, 0),
+   (3, 7, 0),
    (11, 1, 0),
-   (7, 1, 0),
-   (7, 11, 0),
+   (3, 6, 0),
+   (3, 11, 0),
+   (9, 3, 0),
+   (9, 6, 0),
+   (9, 1, 1),
    (2, 11, 0),
-   (2, 4, 0),
-   (6, 11, 0),
-   (6, 10, 1),
-   (6, 4, 0),
-   (5, 0, 1),
-   (9, 4, 1),
-   (9, 1, 0),
-   (9, 0, 0),
-   (9, 7, 0),
+   (4, 3, 0),
+   (2, 0, 0),
+   (4, 0, 1),
+   (2, 7, 0),
+   (2, 6, 1),
+   (4, 11, 0),
+   (4, 9, 0),
+   (4, 7, 0),
+   (8, 4, 1),
+   (8, 6, 0),
+   (8, 3, 0),
+   (5, 8, 1),
+   (5, 7, 0),
    (5, 11, 0),
-   (5, 7, 0),
-   (5, 1, 0),
-   (5, 2, 1),
-   (5, 6, 0),
-   (8, 5, 1),
-   (8, 7, 0),
-   (8, 1, 0),
-   (8, 2, 1),
+   (5, 4, 1),
 )
 ARRIVALS = (
-    ((1, 0), (3, 0), (4, 0), (10, 0), (1, 1), (3, 1), (4, 1), (10, 1), (7, 0), (11, 0), (1, 2), (3, 2), (4, 2), (10, 2), (7, 1), (11, 1), (1, 3), (3, 3), (4, 3), (10, 3),),
-    ((7, 2), (11, 2),),
-    (),
-    ((2, 0), (2, 1), (5, 0), (9, 0),),
-    ((7, 3), (11, 3),),
-    (),
-    ((2, 2), (5, 1), (9, 1), (6, 2),),
-    (),
-    ((6, 0), (8, 0), (2, 3), (5, 2), (9, 2), (6, 3),),
-    ((6, 1), (8, 1),),
-    ((5, 3), (9, 3),),
-    (),
+    ((1, 2), (6, 2), (7, 2), (10, 0), (1, 3), (6, 3), (7, 3), (10, 1), (3, 2), (11, 0), (1, 0), (6, 0), (7, 0), (10, 2), (3, 3), (11, 1), (1, 1), (6, 1), (7, 1), (10, 3),),
+    (),
+    (),
+    ((3, 0), (11, 2), (2, 2), (4, 2), (8, 3), (9, 0),),
+    ((3, 1), (11, 3),),
+    ((2, 3), (4, 3), (8, 0), (9, 1),),
+    (),
+    (),
+    ((5, 2), (9, 3), (2, 0), (4, 0), (8, 1), (9, 2),),
+    ((5, 3), (2, 1), (4, 1),),
+    (),
+    (),
+    ((5, 0),),
     ((8, 2),),
     (),
-    (),
-    ((8, 3),),
+    ((5, 1),),
     (),
     (),
 )
@@ -172,6 +173,17 @@
     return None
 
 
+SAME_CORE = {tile: place for place, tile in enumerate(range(1, COUNT))}
+CROSS_CORE = {tile: len(SAME_CORE) + place for place, tile in enumerate(COL_TILES)}
+MESSAGES = len(SAME_CORE) + len(CROSS_CORE)
+SAME_CORE[0] = MESSAGES
+
+
+def done_round(tile):
+    last = max([n for n, (x, y, one) in enumerate(PAIRS) if x == tile or (y == tile and not one)], default=0)
+    return min(last // 2 + (2 if last % 2 else 1), ROUNDS)
+
+
 def kernel(
     cand_ref, embed_ref, counts_ref, tops_ref, recount_ref,
     tiles, near, far, row_sums, row_tops, kept_sums, col_sums, col_tops,
@@ -180,16 +192,21 @@
 ):
     my_row = lax.axis_index("row")
     my_col = lax.axis_index("col")
-    z, x_hi = my_row // 2, my_row % 2
-    y, x_lo, core = my_col // 4, (my_col // 2) % 2, my_col % 2
+    z, x_hi = lax.div(my_row, 2), lax.rem(my_row, 2)
+    y, x_lo, core = lax.div(my_col, 4), lax.rem(lax.div(my_col, 2), 2), lax.rem(my_col, 2)
     x = x_hi * 2 + x_lo
     other = 1 - core
+    chips = {}
+    for offset in TILES + DIRECTIONS:
+        if offset not in chips:
+            px = lax.rem(x + offset[0], 4)
+            py = lax.rem(y + offset[1], 4)
+            pz = lax.rem(z + offset[2], 4)
+            chips[offset] = (pz * 2 + lax.div(px, 2), py * 4 + lax.rem(px, 2) * 2)
 
     def device(offset, at_core):
-        px = (x + offset[0]) % 4
-        py = (y + offset[1]) % 4
-        pz = (z + offset[2]) % 4
-        return (pz * 2 + px // 2, py * 4 + (px % 2) * 2 + at_core)
+        row, col = chips[offset]
+        return (row, col + at_core)
 
     def span(chunk):
         return pl.ds(chunk * PIECE, PIECE)
@@ -201,7 +218,7 @@
         return pltpu.make_async_remote_copy(
             src_ref=source,
             dst_ref=tiles.at[tile, core, span(chunk)],
-            send_sem=hop_send.at[tile, chunk],
+            send_sem=hop_send,
             recv_sem=hop_recv.at[tile, chunk],
             device_id=device(minus((0, 0, 0), step), core),
             device_id_type=MESH,
@@ -212,7 +229,7 @@
         return pltpu.make_async_remote_copy(
             src_ref=source,
             dst_ref=tiles.at[tile, core, span(chunk)],
-            send_sem=twin_send.at[tile],
+            send_sem=twin_send,
             recv_sem=twin_recv.at[tile],
             device_id=device((0, 0, 0), other),
             device_id_type=MESH,
@@ -222,29 +239,19 @@
         return pltpu.make_async_remote_copy(
             src_ref=tiles.at[tile, other],
             dst_ref=tiles.at[tile, other],
-            send_sem=twin_send.at[tile],
+            send_sem=twin_send,
             recv_sem=twin_recv.at[tile],
             device_id=device((0, 0, 0), other),
             device_id_type=MESH,
         )
 
-    def post(tile, at_core):
+    def post(tile, place, at_core):
         return pltpu.make_async_remote_copy(
-            src_ref=outbox.at[tile, at_core],
-            dst_ref=inbox.at[tile, core],
-            send_sem=post_send.at[tile, at_core],
-            recv_sem=post_recv.at[tile, core],
+            src_ref=outbox.at[place],
+            dst_ref=inbox.at[place],
+            send_sem=post_send,
+            recv_sem=post_recv,
             device_id=device(TILES[tile], at_core),
-            device_id_type=MESH,
-        )
-
-    def posted(tile, from_core):
-        return pltpu.make_async_remote_copy(
-            src_ref=outbox.at[tile, from_core],
-            dst_ref=inbox.at[tile, from_core],
-            send_sem=post_send.at[tile, from_core],
-            recv_sem=post_recv.at[tile, from_core],
-            device_id=device(TILES[tile], from_core),
             device_id_type=MESH,
         )
 
@@ -257,9 +264,8 @@
     pl.semaphore_signal(barrier, inc=1, device_id=device((0, 0, 0), other), device_id_type=MESH)
     pl.semaphore_wait(barrier, 7)
 
-    for chunk in range(CHUNKS):
-        for tile, piece in CHILDREN.get((0, chunk), ()):
-            hop(tile, piece).start()
+    for tile, chunk in FIRST:
+        hop(tile, chunk).start()
     for chunk in range(CHUNKS):
         twin(0, chunk).start()
 
@@ -320,6 +326,41 @@
     multiply(near, 0, 0)
     reduce(near, 0, SPARE_KEPT + 1, SPARE_COL, own_pair=True)
 
+    def across(values, op):
+        return op(values.T, axis=0, keepdims=True)
+
+    def column(values, op, half):
+        mine = jnp.where(core == half, values[:, :ROWS], values[:, ROWS:])
+        return op(mine, axis=0, keepdims=True)
+
+    def finish(tile):
+        places = {0: SAME_CORE[tile]}
+        if tile in COL_TILES:
+            places[1] = CROSS_CORE[tile]
+        for half, place in reversed(places.items()):
+            sums = tops = None
+            if tile in COL_TILES:
+                sums = column(col_sums[tile], jnp.sum, half)
+                tops = column(col_tops[tile], jnp.max, half)
+            for at, (_, _, right) in enumerate(KEPT):
+                if right is not None and right[0] == tile:
+                    extra = column(col_sums[KEPT_COL + at], jnp.sum, half)
+                    sums = sums + extra
+                    tops = jnp.maximum(tops, column(col_tops[KEPT_COL + at], jnp.max, half))
+                    if half == 0:
+                        outbox[place, pl.ds(right[1], 1), :] = extra
+            if half == 0 and (tile in ROW_TILES or tile == 0):
+                low, high = across(row_sums[tile], jnp.sum), across(row_tops[tile], jnp.max)
+                sums = low if sums is None else sums + low
+                tops = high if tops is None else jnp.maximum(tops, high)
+                for at, (_, left, _) in enumerate(KEPT):
+                    if left[0] == tile:
+                        outbox[place, pl.ds(left[1], 1), :] = across(kept_sums[at], jnp.sum)
+            outbox[place, 0:1, :] = sums
+            outbox[place, 1:2, :] = tops
+            if place != MESSAGES:
+                post(tile, place, other if half else core).start()
+
     def arrivals(number):
         def run():
             for tile, chunk in ARRIVALS[number]:
@@ -327,6 +368,9 @@
             for tile in SHARED_TILES:
                 if tile != 0 and first_use(tile) == number:
                     twin_whole(tile).wait_recv()
+            for tile in range(COUNT):
+                if done_round(tile) == number:
+                    finish(tile)
             values = []
             for step in (2 * number, 2 * number + 1):
                 values += slots(step) if step < len(PAIRS) else NOTHING
@@ -345,76 +389,34 @@
         0, ROUNDS, round_of, tuple(jnp.int32(v) for v in NOTHING[2:5])
     )
     reduce(far, *last)
-
-    def across(values, op):
-        return op(values.T, axis=0, keepdims=True)
-
-    sends = []
     for tile in list(range(1, COUNT)) + [0]:
-        for at_core in (0, 1):
-            lanes = pl.ds(at_core * ROWS, ROWS)
-            sums = jnp.zeros((1, ROWS), jnp.float32)
-            tops = jnp.full((1, ROWS), LOWEST, jnp.float32)
-            if tile in COL_TILES:
-                sums = jnp.sum(col_sums[tile, :, lanes], axis=0, keepdims=True)
-                tops = jnp.max(col_tops[tile, :, lanes], axis=0, keepdims=True)
-            for place, (_, _, right) in enumerate(KEPT):
-                if right is not None and right[0] == tile:
-                    extra = jnp.sum(col_sums[KEPT_COL + place, :, lanes], axis=0, keepdims=True)
-                    sums = sums + extra
-                    outbox[tile, at_core, pl.ds(right[1], 1), :] = extra
-                    tops = jnp.maximum(
-                        tops, jnp.max(col_tops[KEPT_COL + place, :, lanes], axis=0, keepdims=True)
-                    )
-            outbox[tile, at_core, 0:1, :] = sums
-            outbox[tile, at_core, 1:2, :] = tops
-        if tile in ROW_TILES or tile == 0:
-            outbox[tile, core, 0:1, :] += across(row_sums[tile], jnp.sum)
-            outbox[tile, core, 1:2, :] = jnp.maximum(
-                outbox[tile, core, 1:2, :], across(row_tops[tile], jnp.max)
-            )
-        for place, (_, left, _) in enumerate(KEPT):
-            if left[0] == tile:
-                outbox[tile, core, pl.ds(left[1], 1), :] = across(kept_sums[place], jnp.sum)
-        if tile != 0:
-            post(tile, core).start()
-        if tile in COL_TILES:
-            post(tile, other).start()
+        if done_round(tile) == ROUNDS:
+            finish(tile)
     table[0:1, :] = across(kept_sums[SPARE_KEPT + 1], jnp.sum)
 
-    sums = outbox[0, core, 0:1, :]
-    tops = outbox[0, core, 1:2, :]
-    for tile in list(range(1, COUNT)) + [0]:
-        for from_core in (core, other):
-            if from_core is core and tile == 0:
-                continue
-            if from_core is other and tile not in COL_TILES:
-                continue
-            posted(tile, from_core).wait_recv()
-            sums = sums + inbox[tile, from_core, 0:1, :]
-            tops = jnp.maximum(tops, inbox[tile, from_core, 1:2, :])
-    counts_ref[...] = sums
-    tops_ref[...] = tops
+    moved = tiles.at[pl.ds(1, COUNT - 1), core]
+    pltpu.make_async_copy(moved, moved, hop_send).wait()
+    shared = tiles.at[pl.ds(0, len(SHARED_TILES)), core]
+    pltpu.make_async_copy(shared, shared, twin_send).wait()
+    sent = outbox.at[pl.ds(0, MESSAGES)]
+    pltpu.make_async_copy(sent, sent, post_send).wait()
+    pltpu.make_async_copy(inbox, inbox, post_recv).wait()
+
+    sums = tops = outbox[MESSAGES]
+    for place in range(MESSAGES):
+        sums = sums + inbox[place]
+        tops = jnp.maximum(tops, inbox[place])
+    counts_ref[...] = sums[0:1, :]
+    tops_ref[...] = tops[1:2, :]
     for _, left, right in KEPT:
         for side in (left, right):
             if side is not None:
                 where = outbox if side[0] == 0 else inbox
-                table[pl.ds(side[2], 1), :] = where[side[0], core, pl.ds(side[1], 1), :]
+                table[pl.ds(side[2], 1), :] = where[SAME_CORE[side[0]], pl.ds(side[1], 1), :]
     for number in range(2):
         chosen = cand_ref[number]
         apart = ((chosen // 2 - z + 4) % 4) * 2 + (chosen % 2 - x_hi + 2) % 2
         recount_ref[pl.ds(number, 1), :] = table[pl.ds(apart, 1), :]
-
-    for tile in range(1, COUNT):
-        for chunk in range(CHUNKS):
-            hop(tile, chunk).wait_send()
-    for tile in SHARED_TILES:
-        twin_whole(tile).wait_send()
-    for tile in range(COUNT):
-        if tile != 0:
-            post(tile, core).wait_send()
-        if tile in COL_TILES:
-            post(tile, other).wait_send()
 
 
 def per_device(embed, cand_tiles):
@@ -441,16 +443,16 @@
             vector((SPARE_KEPT + 2, ROWS, 128), jnp.float32),
             vector((KEPT_COL + len(KEPT), 8, 2 * ROWS), jnp.float32),
             vector((KEPT_COL + len(KEPT), 8, 2 * ROWS), jnp.float32),
-            vector((COUNT, 2, 8, ROWS), jnp.float32),
-            vector((COUNT, 2, 8, ROWS), jnp.float32),
+            vector((MESSAGES + 1, 8, ROWS), jnp.float32),
+            vector((MESSAGES, 8, ROWS), jnp.float32),
             vector((8, ROWS), jnp.float32),
             semaphores,
+            semaphores,
             semaphores((COUNT, CHUNKS)),
-            semaphores((COUNT, CHUNKS)),
+            semaphores,
             semaphores((COUNT,)),
-            semaphores((COUNT,)),
-            semaphores((COUNT, 2)),
-            semaphores((COUNT, 2)),
+            semaphores,
+            semaphores,
         ],
         compiler_params=pltpu.CompilerParams(
             collective_id=0, has_side_effects=True, vmem_limit_bytes=56 * 1024 * 1024

time: 50.6 us -> 47.1 us (0.931); the launches traced: 50.5 us -> 46.4 us
  Pallas kernels: 47.5 us -> 43.4 us
    pallas_call x1, Pallas kernels: 47.5 us -> 43.4 us  [per_device(): pl.pallas_call(kernel, out_shape=(jax.ShapeDtypeStruct((1, ROWS), jnp.flo...]
where the time goes in v2:
time: 47.1 us; the launch traced here: 46.4 us
  Pallas kernels  43.4 us (92%)
  local copies, waits for them, and re-layouts  2.33 us (5%)
  between operations  0.66 us (1%)
    pallas_call x1, Pallas kernels, per_device(): pl.pallas_call(kernel, out_shape=(jax.ShapeDtypeStruct((1, ROWS), jnp.flo...  43.4 us
    unnamed x9, local copies, waits for them, and re-layouts  2.33 us

profile of v2, /device:TPU:1, one launch (start us, length us, event | category | flops | bytes accessed | tf_op | source)
XLA Modules:
  0.0 46.4 jit_solution(6191833755628412551)
XLA Ops:
  0.6 43.4 %shard_map.49 = (f32[1,256]{1,0:T(1,128)}, f32[1,256]{1,0:T(1,128)}, f32[2,256]{1,0:T(2,128)}) custom-call(s32[2]{0:T(128)} %cand_ref.1, bf16[256,768]{1,0:T(8,128)(2,1)} %embed_ref.1), custom_call_target="tpu_custom_call" | custom-call | flops 7449083904 | bytes 9437184 | tf_op jit(solution)/shard_map/pallas_call | solution.py:425
  44.0 0.0 copy-start.2
  44.0 0.0 copy-start.1
  44.0 0.6 %copy-done.2 = f32[1,256]{1,0:T(1,128)S(1)} copy-done((f32[1,256]{1,0:T(1,128)S(1)}, f32[1,256]{1,0:T(1,128)}, u32[]{:S(2)}) %copy-start.2) | copy-done | bytes 1048
  44.6 0.0 copy-start
  44.6 0.6 %copy.8 = f32[256]{0:T(256)} copy(f32[256]{0:T(256)S(1)} %bitcast.3) | data formatting | bytes 2048
  45.2 0.0 copy-done.1
  45.2 0.6 %copy.9 = f32[256]{0:T(256)} copy(f32[256]{0:T(256)S(1)} %bitcast.2) | data formatting | bytes 2048
  45.8 0.0 copy-done
  45.8 0.6 %copy.10 = f32[2,256]{1,0:T(2,128)} copy(f32[2,256]{1,0:T(2,128)S(1)} %copy-done) | data formatting | bytes 4096
Async XLA Ops:
  44.0 0.6 %copy-start.2 = (f32[1,256]{1,0:T(1,128)S(1)}, f32[1,256]{1,0:T(1,128)}, u32[]{:S(2)}) copy-start(f32[1,256]{1,0:T(1,128)} %get-tuple-element.6) | copy-start | bytes 3076
  44.0 1.2 %copy-start.1 = (f32[1,256]{1,0:T(1,128)S(1)}, f32[1,256]{1,0:T(1,128)}, u32[]{:S(2)}) copy-start(f32[1,256]{1,0:T(1,128)} %get-tuple-element.7) | copy-start | bytes 3076
  44.6 1.1 %copy-start = (f32[2,256]{1,0:T(2,128)S(1)}, f32[2,256]{1,0:T(2,128)}, u32[]{:S(2)}) copy-start(f32[2,256]{1,0:T(2,128)} %get-tuple-element.14) | copy-start | bytes 6148

commit v3 on v2

--- a/solution.py
+++ b/solution.py
@@ -15,87 +15,104 @@
 CHUNKS = 4
 TILES = (
    (0, 0, 0),
-   (0, 0, 3),
-   (0, 1, 2),
+   (0, 0, 1),
+   (0, 1, 0),
    (0, 1, 3),
    (0, 2, 0),
-   (0, 2, 2),
+   (0, 2, 3),
    (0, 3, 0),
    (1, 0, 0),
    (2, 0, 0),
-   (2, 0, 1),
-   (3, 0, 0),
+   (2, 0, 2),
    (3, 0, 1),
+   (3, 0, 2),
 )
 ROUTES = (
     (),
+   (4, 4, 4, 4),
+   (2, 2, 2, 2),
    (5, 5, 5, 5),
-   (5, 5, 5, 5),
-   (2, 2, 2, 2),
-   (3, 3, 3, 3),
-   (2, 2, 2, 2),
+   (3, 3, 4, 3),
+   (2, 2, 2, 5),
    (3, 3, 3, 3),
    (0, 0, 0, 0),
-   (0, 0, 5, 0),
-   (1, 1, 1, 4),
+   (0, 0, 0, 0),
+   (1, 1, 1, 1),
    (1, 1, 1, 1),
    (4, 4, 4, 4),
 )
-FIRST = ((1, 2), (6, 2), (7, 2), (10, 0), (1, 3), (6, 3), (7, 3), (10, 1), (1, 0), (6, 0), (7, 0), (10, 2), (1, 1), (6, 1), (7, 1), (10, 3),)
+FIRST = ((1, 2), (2, 0), (6, 2), (7, 0), (1, 3), (2, 1), (6, 3), (7, 1), (1, 0), (2, 2), (6, 0), (7, 2), (1, 1), (2, 3), (6, 1), (7, 3),)
 PAIRS = (
    (1, 0, 0),
-   (6, 0, 0),
+   (2, 0, 0),
    (7, 0, 0),
-   (7, 10, 1),
    (1, 6, 0),
-   (6, 10, 0),
+   (1, 2, 0),
+   (2, 6, 1),
+   (2, 7, 0),
+   (6, 7, 0),
    (1, 7, 0),
-   (6, 7, 0),
-   (1, 10, 0),
+   (10, 2, 0),
+   (10, 7, 0),
+   (10, 6, 0),
+   (3, 7, 0),
+   (3, 1, 0),
+   (3, 6, 0),
    (3, 10, 0),
-   (11, 7, 0),
+   (5, 7, 0),
+   (5, 10, 0),
+   (5, 1, 1),
+   (8, 3, 0),
+   (11, 0, 0),
+   (8, 5, 0),
+   (8, 2, 0),
+   (11, 7, 1),
+   (8, 0, 1),
    (11, 6, 0),
-   (3, 7, 0),
-   (11, 1, 0),
-   (3, 6, 0),
-   (3, 11, 0),
+   (8, 10, 0),
+   (11, 3, 0),
+   (4, 10, 0),
+   (4, 7, 0),
+   (4, 8, 1),
+   (9, 4, 1),
+   (9, 2, 0),
    (9, 3, 0),
-   (9, 6, 0),
-   (9, 1, 1),
-   (2, 11, 0),
-   (4, 3, 0),
-   (2, 0, 0),
-   (4, 0, 1),
-   (2, 7, 0),
-   (2, 6, 1),
-   (4, 11, 0),
-   (4, 9, 0),
-   (4, 7, 0),
-   (8, 4, 1),
-   (8, 6, 0),
-   (8, 3, 0),
-   (5, 8, 1),
-   (5, 7, 0),
-   (5, 11, 0),
-   (5, 4, 1),
+   (9, 8, 1),
 )
 ARRIVALS = (
-    ((1, 2), (6, 2), (7, 2), (10, 0), (1, 3), (6, 3), (7, 3), (10, 1), (3, 2), (11, 0), (1, 0), (6, 0), (7, 0), (10, 2), (3, 3), (11, 1), (1, 1), (6, 1), (7, 1), (10, 3),),
-    (),
-    (),
-    ((3, 0), (11, 2), (2, 2), (4, 2), (8, 3), (9, 0),),
-    ((3, 1), (11, 3),),
-    ((2, 3), (4, 3), (8, 0), (9, 1),),
-    (),
-    (),
-    ((5, 2), (9, 3), (2, 0), (4, 0), (8, 1), (9, 2),),
-    ((5, 3), (2, 1), (4, 1),),
-    (),
-    (),
-    ((5, 0),),
-    ((8, 2),),
-    (),
-    ((5, 1),),
+    ((1, 2), (2, 0), (6, 2), (7, 0), (1, 3), (2, 1), (6, 3), (7, 1), (3, 0), (10, 2), (1, 0), (2, 2), (6, 0), (7, 2), (3, 1), (10, 3), (1, 1), (2, 3), (6, 1), (7, 3),),
+    (),
+    (),
+    (),
+    (),
+    ((3, 2), (10, 0), (4, 3), (5, 0), (8, 0), (11, 2),),
+    (),
+    (),
+    (),
+    ((3, 3), (10, 1), (4, 0), (5, 1), (8, 1), (11, 3),),
+    (),
+    (),
+    (),
+    (),
+    (),
+    ((5, 3), (9, 2), (4, 1), (5, 2), (8, 2), (11, 0),),
+    (),
+    (),
+    (),
+    ((9, 3), (8, 3), (11, 1),),
+    (),
+    (),
+    (),
+    (),
+    ((9, 0),),
+    ((4, 2),),
+    (),
+    (),
+    (),
+    (),
+    (),
+    ((9, 1),),
+    (),
     (),
     (),
 )
@@ -169,7 +186,7 @@
 def first_use(tile):
     for number, (_, y, _) in enumerate(PAIRS):
         if y == tile:
-            return number // 2
+            return number
     return None
 
 
@@ -179,15 +196,52 @@
 SAME_CORE[0] = MESSAGES
 
 
+def last_round(tile, cols):
+    steps = [n for n, (x, y, one) in enumerate(PAIRS) if x == tile or (cols and y == tile and not one)]
+    last = max(steps, default=-1)
+    return 0 if last < 0 else last // 2 + last % 2
+
+
+def lane_rounds():
+    rows, kept, free = {}, {}, {}
+    for tile in sorted(ROW_TILES + ([] if 0 in ROW_TILES else [0]), key=lambda t: last_round(t, False)):
+        at = last_round(tile, False) + 1
+        while at in free:
+            at += 1
+        free[at] = tile
+        rows[tile] = at
+    used = set()
+    for place, (number, _, _) in enumerate(KEPT):
+        at = number // 2 + number % 2 + 1
+        while at in used:
+            at += 1
+        used.add(at)
+        kept[place] = at
+    return rows, kept
+
+
+LANE_ROWS, LANE_KEPT = lane_rounds()
+
+
 def done_round(tile):
-    last = max([n for n, (x, y, one) in enumerate(PAIRS) if x == tile or (y == tile and not one)], default=0)
-    return min(last // 2 + (2 if last % 2 else 1), ROUNDS)
+    at = last_round(tile, True) + 1
+    if LANE_ROWS.get(tile, -1) < ROUNDS:
+        at = max(at, LANE_ROWS.get(tile, -1) + 1)
+    for place, (_, left, _) in enumerate(KEPT):
+        if left[0] == tile and LANE_KEPT[place] < ROUNDS:
+            at = max(at, LANE_KEPT[place] + 1)
+    if LANE_ROWS.get(tile, -1) >= ROUNDS:
+        at = ROUNDS
+    for place, (_, left, _) in enumerate(KEPT):
+        if left[0] == tile and LANE_KEPT[place] >= ROUNDS:
+            at = ROUNDS
+    return min(at, ROUNDS)
 
 
 def kernel(
     cand_ref, embed_ref, counts_ref, tops_ref, recount_ref,
     tiles, near, far, row_sums, row_tops, kept_sums, col_sums, col_tops,
-    outbox, inbox, table,
+    row_lanes, kept_lanes, outbox, inbox, table,
     own_sem, hop_send, hop_recv, twin_send, twin_recv, post_send, post_recv,
 ):
     my_row = lax.axis_index("row")
@@ -350,44 +404,58 @@
                     if half == 0:
                         outbox[place, pl.ds(right[1], 1), :] = extra
             if half == 0 and (tile in ROW_TILES or tile == 0):
-                low, high = across(row_sums[tile], jnp.sum), across(row_tops[tile], jnp.max)
+                if LANE_ROWS[tile] < ROUNDS:
+                    low, high = row_lanes[tile, 0:1, :], row_lanes[tile, 1:2, :]
+                else:
+                    low, high = across(row_sums[tile], jnp.sum), across(row_tops[tile], jnp.max)
                 sums = low if sums is None else sums + low
                 tops = high if tops is None else jnp.maximum(tops, high)
                 for at, (_, left, _) in enumerate(KEPT):
                     if left[0] == tile:
-                        outbox[place, pl.ds(left[1], 1), :] = across(kept_sums[at], jnp.sum)
+                        if LANE_KEPT[at] < ROUNDS:
+                            kept = kept_lanes[at, 0:1, :]
+                        else:
+                            kept = across(kept_sums[at], jnp.sum)
+                        outbox[place, pl.ds(left[1], 1), :] = kept
             outbox[place, 0:1, :] = sums
             outbox[place, 1:2, :] = tops
             if place != MESSAGES:
                 post(tile, place, other if half else core).start()
 
-    def arrivals(number):
-        def run():
-            for tile, chunk in ARRIVALS[number]:
-                arrive(tile, chunk)
-            for tile in SHARED_TILES:
-                if tile != 0 and first_use(tile) == number:
-                    twin_whole(tile).wait_recv()
-            for tile in range(COUNT):
-                if done_round(tile) == number:
-                    finish(tile)
-            values = []
-            for step in (2 * number, 2 * number + 1):
-                values += slots(step) if step < len(PAIRS) else NOTHING
-            return tuple(jnp.int32(v) for v in values)
-        return run
-
-    def round_of(number, before):
-        now = lax.switch(number, [arrivals(n) for n in range(ROUNDS)])
-        multiply(near, now[0], now[1])
+    def lanes(row, kept):
+        row_lanes[row, 0:1, :] = across(row_sums[row], jnp.sum)
+        row_lanes[row, 1:2, :] = across(row_tops[row], jnp.max)
+        kept_lanes[kept, 0:1, :] = across(kept_sums[kept], jnp.sum)
+
+    def arrivals(number, second):
+        if True:
+            step = 2 * number + second
+            if step < len(PAIRS):
+                for tile, chunk in ARRIVALS[step]:
+                    arrive(tile, chunk)
+                for tile in SHARED_TILES:
+                    if tile != 0 and first_use(tile) == step:
+                        twin_whole(tile).wait_recv()
+            values = slots(step) if step < len(PAIRS) else NOTHING
+            if not second:
+                row = [tile for tile, at in LANE_ROWS.items() if at == number] or [SPARE_ROW]
+                kept = [place for place, at in LANE_KEPT.items() if at == number] or [SPARE_KEPT]
+                values = values + (row[0], kept[0])
+                for tile in range(COUNT):
+                    if done_round(tile) == number:
+                        finish(tile)
+            return values
+
+    before = NOTHING[2:5]
+    for number in range(ROUNDS):
+        one, two = arrivals(number, 0), arrivals(number, 1)
+        lanes(*one[5:7])
+        multiply(near, one[0], one[1])
         reduce(far, *before)
-        multiply(far, now[5], now[6])
-        reduce(near, *now[2:5])
-        return tuple(now[7:10])
-
-    last = lax.fori_loop(
-        0, ROUNDS, round_of, tuple(jnp.int32(v) for v in NOTHING[2:5])
-    )
+        multiply(far, two[0], two[1])
+        reduce(near, *one[2:5])
+        before = two[2:5]
+    last = before
     reduce(far, *last)
     for tile in list(range(1, COUNT)) + [0]:
         if done_round(tile) == ROUNDS:
@@ -443,6 +511,8 @@
             vector((SPARE_KEPT + 2, ROWS, 128), jnp.float32),
             vector((KEPT_COL + len(KEPT), 8, 2 * ROWS), jnp.float32),
             vector((KEPT_COL + len(KEPT), 8, 2 * ROWS), jnp.float32),
+            vector((COUNT + 1, 8, ROWS), jnp.float32),
+            vector((SPARE_KEPT + 1, 8, ROWS), jnp.float32),
             vector((MESSAGES + 1, 8, ROWS), jnp.float32),
             vector((MESSAGES, 8, ROWS), jnp.float32),
             vector((8, ROWS), jnp.float32),

time: 47.1 us -> 43.9 us (0.932); the launches traced: 46.4 us -> 43.7 us
  Pallas kernels: 43.4 us -> 40.8 us
    pallas_call x1, Pallas kernels: 43.4 us -> 40.8 us  [per_device(): pl.pallas_call(kernel, out_shape=(jax.ShapeDtypeStruct((1, ROWS), jnp.flo...]
where the time goes in v3:
time: 43.9 us; the launch traced here: 43.7 us
  Pallas kernels  40.8 us (93%)
  local copies, waits for them, and re-layouts  2.33 us (5%)
  between operations  0.66 us (2%)
    pallas_call x1, Pallas kernels, per_device(): pl.pallas_call(kernel, out_shape=(jax.ShapeDtypeStruct((1, ROWS), jnp.flo...  40.8 us
    unnamed x9, local copies, waits for them, and re-layouts  2.33 us

profile of v3, /device:TPU:1, one launch (start us, length us, event | category | flops | bytes accessed | tf_op | source)
XLA Modules:
  0.0 43.7 jit_solution(238558434336212906)
XLA Ops:
  0.6 40.8 %shard_map.49 = (f32[1,256]{1,0:T(1,128)}, f32[1,256]{1,0:T(1,128)}, f32[2,256]{1,0:T(2,128)}) custom-call(s32[2]{0:T(128)} %cand_ref.1, bf16[256,768]{1,0:T(8,128)(2,1)} %embed_ref.1), custom_call_target="tpu_custom_call" | custom-call | flops 7449083904 | bytes 9437184 | tf_op jit(solution)/shard_map/pallas_call | solution.py:493
  41.4 0.0 copy-start.2
  41.4 0.0 copy-start.1
  41.4 0.6 %copy-done.2 = f32[1,256]{1,0:T(1,128)S(1)} copy-done((f32[1,256]{1,0:T(1,128)S(1)}, f32[1,256]{1,0:T(1,128)}, u32[]{:S(2)}) %copy-start.2) | copy-done | bytes 1048
  42.0 0.0 copy-start
  42.0 0.6 %copy.8 = f32[256]{0:T(256)} copy(f32[256]{0:T(256)S(1)} %bitcast.3) | data formatting | bytes 2048
  42.6 0.0 copy-done.1
  42.6 0.6 %copy.9 = f32[256]{0:T(256)} copy(f32[256]{0:T(256)S(1)} %bitcast.2) | data formatting | bytes 2048
  43.2 0.0 copy-done
  43.2 0.6 %copy.10 = f32[2,256]{1,0:T(2,128)} copy(f32[2,256]{1,0:T(2,128)S(1)} %copy-done) | data formatting | bytes 4096
Async XLA Ops:
  41.4 0.6 %copy-start.2 = (f32[1,256]{1,0:T(1,128)S(1)}, f32[1,256]{1,0:T(1,128)}, u32[]{:S(2)}) copy-start(f32[1,256]{1,0:T(1,128)} %get-tuple-element.6) | copy-start | bytes 3076
  41.4 1.2 %copy-start.1 = (f32[1,256]{1,0:T(1,128)S(1)}, f32[1,256]{1,0:T(1,128)}, u32[]{:S(2)}) copy-start(f32[1,256]{1,0:T(1,128)} %get-tuple-element.7) | copy-start | bytes 3076
  42.0 1.1 %copy-start = (f32[2,256]{1,0:T(2,128)S(1)}, f32[2,256]{1,0:T(2,128)}, u32[]{:S(2)}) copy-start(f32[2,256]{1,0:T(2,128)} %get-tuple-element.14) | copy-start | bytes 6148

commit v4 on v3

--- a/solution.py
+++ b/solution.py
@@ -239,9 +239,9 @@
 
 
 def kernel(
-    cand_ref, embed_ref, counts_ref, tops_ref, recount_ref,
+    embed_ref, total_ref, high_ref, table,
     tiles, near, far, row_sums, row_tops, kept_sums, col_sums, col_tops,
-    row_lanes, kept_lanes, outbox, inbox, table,
+    row_lanes, kept_lanes, outbox, inbox,
     own_sem, hop_send, hop_recv, twin_send, twin_recv, post_send, post_recv,
 ):
     my_row = lax.axis_index("row")
@@ -474,34 +474,34 @@
     for place in range(MESSAGES):
         sums = sums + inbox[place]
         tops = jnp.maximum(tops, inbox[place])
-    counts_ref[...] = sums[0:1, :]
-    tops_ref[...] = tops[1:2, :]
+    total_ref[...] = sums
+    high_ref[...] = tops
     for _, left, right in KEPT:
         for side in (left, right):
             if side is not None:
                 where = outbox if side[0] == 0 else inbox
                 table[pl.ds(side[2], 1), :] = where[SAME_CORE[side[0]], pl.ds(side[1], 1), :]
+
+def finisher(cand_ref, total_ref, high_ref, table_ref, counts_ref, tops_ref, recount_ref):
+    my_row = lax.axis_index("row")
+    z, x_hi = my_row // 2, my_row % 2
+    counts_ref[...] = total_ref[0, :]
+    tops_ref[...] = high_ref[1, :]
     for number in range(2):
         chosen = cand_ref[number]
         apart = ((chosen // 2 - z + 4) % 4) * 2 + (chosen % 2 - x_hi + 2) % 2
-        recount_ref[pl.ds(number, 1), :] = table[pl.ds(apart, 1), :]
+        recount_ref[pl.ds(number, 1), :] = table_ref[pl.ds(apart, 1), :]
 
 
 def per_device(embed, cand_tiles):
     vector = pltpu.VMEM
     semaphores = pltpu.SemaphoreType.DMA
-    counts, tops, recount = pl.pallas_call(
+    in_vector = pl.BlockSpec(memory_space=pltpu.VMEM)
+    parts = pl.pallas_call(
         kernel,
-        out_shape=(
-            jax.ShapeDtypeStruct((1, ROWS), jnp.float32),
-            jax.ShapeDtypeStruct((1, ROWS), jnp.float32),
-            jax.ShapeDtypeStruct((2, ROWS), jnp.float32),
-        ),
-        in_specs=[
-            pl.BlockSpec(memory_space=pltpu.SMEM),
-            pl.BlockSpec(memory_space=pl.ANY),
-        ],
-        out_specs=[pl.BlockSpec(memory_space=pltpu.VMEM)] * 3,
+        out_shape=(jax.ShapeDtypeStruct((8, ROWS), jnp.float32),) * 3,
+        in_specs=[pl.BlockSpec(memory_space=pl.ANY)],
+        out_specs=[in_vector] * 3,
         scratch_shapes=[
             vector((COUNT, 2, ROWS, WIDTH), jnp.bfloat16),
             vector((ROWS, 2 * ROWS), jnp.float32),
@@ -515,7 +515,6 @@
             vector((SPARE_KEPT + 1, 8, ROWS), jnp.float32),
             vector((MESSAGES + 1, 8, ROWS), jnp.float32),
             vector((MESSAGES, 8, ROWS), jnp.float32),
-            vector((8, ROWS), jnp.float32),
             semaphores,
             semaphores,
             semaphores((COUNT, CHUNKS)),
@@ -532,8 +531,17 @@
             bytes_accessed=COUNT * 2 * ROWS * WIDTH * 2,
             transcendentals=37 * ROWS * 2 * ROWS,
         ),
-    )(cand_tiles, embed)
-    return counts.reshape(ROWS), tops.reshape(ROWS), recount
+    )(embed)
+    return pl.pallas_call(
+        finisher,
+        out_shape=(
+            jax.ShapeDtypeStruct((ROWS,), jnp.float32),
+            jax.ShapeDtypeStruct((ROWS,), jnp.float32),
+            jax.ShapeDtypeStruct((2, ROWS), jnp.float32),
+        ),
+        in_specs=[pl.BlockSpec(memory_space=pltpu.SMEM)] + [in_vector] * 3,
+        out_specs=[in_vector] * 3,
+    )(cand_tiles, *parts)
 
 
 def solution(mesh):

time: 43.9 us -> 42.4 us (0.966)
  local copies, waits for them, and re-layouts: 2.33 us -> 0 us
  Pallas kernels: 40.8 us -> 41.6 us
    unnamed x9 -> x0, local copies, waits for them, and re-layouts: 2.33 us -> none
    pallas_call x1 -> x2, Pallas kernels: 40.8 us -> 41.6 us  [the longest x1 40.1 us: per_device(): pl.pallas_call(kernel, out_shape=(jax.ShapeDtypeStruct((8, ROWS), jnp.flo...]
where the time goes in v4:
time: 42.4 us; the launch traced here: 42.2 us
  Pallas kernels  41.6 us (98%)
  between operations  0.64 us (2%)
    pallas_call x1, Pallas kernels, per_device(): pl.pallas_call(kernel, out_shape=(jax.ShapeDtypeStruct((8, ROWS), jnp.flo...  40.1 us
    pallas_call x1, Pallas kernels, per_device(): pl.pallas_call(finisher, out_shape=(jax.ShapeDtypeStruct((ROWS,), jnp.flo...  1.42 us

profile of v4, /device:TPU:1, one launch (start us, length us, event | category | flops | bytes accessed | tf_op | source)
XLA Modules:
  0.0 42.2 jit_solution(1865845727125642801)
XLA Ops:
  0.6 40.1 %shard_map.49 = (f32[8,256]{1,0:T(8,128)}, f32[8,256]{1,0:T(8,128)}, f32[8,256]{1,0:T(8,128)}) custom-call(bf16[256,768]{1,0:T(8,128)(2,1)} %embed_ref.1), custom_call_target="tpu_custom_call" | custom-call | flops 7449083904 | bytes 9437184 | tf_op jit(solution)/shard_map/pallas_call | solution.py:500
  40.8 1.4 %shard_map.50 = (f32[256]{0:T(256)}, f32[256]{0:T(256)}, f32[2,256]{1,0:T(2,128)}) custom-call(s32[2]{0:T(128)} %cand_ref.1, f32[8,256]{1,0:T(8,128)} %get-tuple-element.6.total_ref, f32[8,256]{1,0:T(8,128)} %get-tuple-element.7.high_ref, f32[8,256]{1,0:T(8,128)} %get-tuple-element.8.table_ref), custom_call_target="tpu_custom_call" | custom-call | tf_op jit(solution)/shard_map/pallas_call | solution.py:535

commit v5 on v4

--- a/solution.py
+++ b/solution.py
@@ -16,97 +16,99 @@
 TILES = (
    (0, 0, 0),
    (0, 0, 1),
+   (0, 0, 2),
    (0, 1, 0),
+   (0, 1, 2),
    (0, 1, 3),
-   (0, 2, 0),
-   (0, 2, 3),
    (0, 3, 0),
    (1, 0, 0),
    (2, 0, 0),
-   (2, 0, 2),
-   (3, 0, 1),
-   (3, 0, 2),
+   (2, 3, 0),
+   (3, 0, 0),
+   (3, 2, 0),
+   (3, 3, 0),
 )
 ROUTES = (
     (),
    (4, 4, 4, 4),
+   (4, 4, 4, 4),
    (2, 2, 2, 2),
+   (5, 2, 2, 5),
    (5, 5, 5, 5),
-   (3, 3, 4, 3),
-   (2, 2, 2, 5),
+   (3, 3, 0, 3),
+   (0, 0, 0, 0),
+   (0, 0, 1, 1),
+   (1, 1, 1, 1),
+   (2, 2, 1, 1),
    (3, 3, 3, 3),
-   (0, 0, 0, 0),
-   (0, 0, 0, 0),
-   (1, 1, 1, 1),
-   (1, 1, 1, 1),
-   (4, 4, 4, 4),
+   (1, 1, 3, 3),
 )
-FIRST = ((1, 2), (2, 0), (6, 2), (7, 0), (1, 3), (2, 1), (6, 3), (7, 1), (1, 0), (2, 2), (6, 0), (7, 2), (1, 1), (2, 3), (6, 1), (7, 3),)
+FIRST = ((1, 0), (3, 2), (6, 0), (7, 2), (10, 2), (1, 1), (3, 3), (6, 1), (7, 3), (10, 3), (1, 2), (3, 0), (6, 3), (7, 0), (1, 3), (3, 1), (7, 1),)
 PAIRS = (
    (1, 0, 0),
-   (2, 0, 0),
+   (3, 0, 0),
    (7, 0, 0),
-   (1, 6, 0),
-   (1, 2, 0),
-   (2, 6, 1),
+   (3, 7, 0),
+   (1, 3, 0),
+   (1, 7, 0),
+   (12, 7, 0),
+   (12, 3, 0),
+   (12, 1, 0),
+   (12, 0, 0),
+   (5, 1, 0),
+   (8, 1, 0),
+   (8, 0, 1),
+   (5, 12, 0),
+   (5, 7, 0),
+   (5, 8, 0),
+   (6, 5, 0),
+   (6, 3, 1),
+   (6, 1, 0),
+   (10, 1, 0),
+   (10, 5, 0),
+   (2, 0, 1),
+   (2, 8, 1),
+   (2, 12, 0),
    (2, 7, 0),
-   (6, 7, 0),
-   (1, 7, 0),
-   (10, 2, 0),
-   (10, 7, 0),
-   (10, 6, 0),
-   (3, 7, 0),
-   (3, 1, 0),
-   (3, 6, 0),
-   (3, 10, 0),
-   (5, 7, 0),
-   (5, 10, 0),
-   (5, 1, 1),
-   (8, 3, 0),
-   (11, 0, 0),
-   (8, 5, 0),
-   (8, 2, 0),
+   (11, 5, 0),
+   (11, 2, 0),
+   (11, 1, 0),
    (11, 7, 1),
-   (8, 0, 1),
-   (11, 6, 0),
-   (8, 10, 0),
-   (11, 3, 0),
-   (4, 10, 0),
    (4, 7, 0),
-   (4, 8, 1),
+   (4, 8, 0),
+   (4, 6, 1),
+   (9, 1, 0),
+   (9, 5, 0),
    (9, 4, 1),
-   (9, 2, 0),
-   (9, 3, 0),
-   (9, 8, 1),
 )
 ARRIVALS = (
-    ((1, 2), (2, 0), (6, 2), (7, 0), (1, 3), (2, 1), (6, 3), (7, 1), (3, 0), (10, 2), (1, 0), (2, 2), (6, 0), (7, 2), (3, 1), (10, 3), (1, 1), (2, 3), (6, 1), (7, 3),),
-    (),
-    (),
-    (),
-    (),
-    ((3, 2), (10, 0), (4, 3), (5, 0), (8, 0), (11, 2),),
-    (),
-    (),
-    (),
-    ((3, 3), (10, 1), (4, 0), (5, 1), (8, 1), (11, 3),),
-    (),
-    (),
-    (),
-    (),
-    (),
-    ((5, 3), (9, 2), (4, 1), (5, 2), (8, 2), (11, 0),),
-    (),
-    (),
-    (),
-    ((9, 3), (8, 3), (11, 1),),
-    (),
-    (),
-    (),
-    (),
-    ((9, 0),),
+    ((1, 0), (3, 2), (6, 0), (7, 2), (10, 2), (1, 1), (3, 3), (6, 1), (7, 3), (10, 3), (1, 2), (3, 0), (6, 3), (7, 0), (5, 2), (12, 0), (1, 3), (3, 1), (7, 1), (12, 2),),
+    ((5, 3), (8, 2),),
+    (),
+    (),
+    (),
+    ((2, 0), (12, 3),),
+    ((5, 0), (8, 0), (12, 1),),
+    ((10, 0),),
+    (),
+    (),
+    ((2, 1), (11, 0), (5, 1), (8, 1), (8, 3),),
+    (),
+    (),
+    (),
+    ((2, 2), (11, 2),),
+    ((4, 3), (6, 2), (9, 0),),
+    ((10, 1),),
+    (),
+    (),
+    ((2, 3), (11, 3),),
+    ((4, 0), (9, 2),),
+    ((4, 1),),
+    (),
+    (),
+    ((11, 1),),
+    ((9, 3),),
     ((4, 2),),
-    (),
     (),
     (),
     (),

time: 42.4 us -> 41.3 us (0.974)
  the two profiles are of different devices: /device:TPU:1 before, /device:TPU:0 now
where the time goes in v5:
time: 41.3 us; the launch traced here: 41.1 us
  Pallas kernels  40.5 us (98%)
  between operations  0.64 us (2%)
    pallas_call x1, Pallas kernels, per_device(): pl.pallas_call(kernel, out_shape=(jax.ShapeDtypeStruct((8, ROWS), jnp.flo...  39.1 us
    pallas_call x1, Pallas kernels, per_device(): pl.pallas_call(finisher, out_shape=(jax.ShapeDtypeStruct((ROWS,), jnp.flo...  1.42 us

profile of v5, /device:TPU:0, one launch (start us, length us, event | category | flops | bytes accessed | tf_op | source)
XLA Modules:
  0.0 41.1 jit_solution(8640276345759128439)
XLA Ops:
  0.6 39.1 %shard_map.49 = (f32[8,256]{1,0:T(8,128)}, f32[8,256]{1,0:T(8,128)}, f32[8,256]{1,0:T(8,128)}) custom-call(bf16[256,768]{1,0:T(8,128)(2,1)} %embed_ref.1), custom_call_target="tpu_custom_call" | custom-call | flops 7449083904 | bytes 10223616 | tf_op jit(solution)/shard_map/pallas_call | solution.py:502
  39.7 1.4 %shard_map.50 = (f32[256]{0:T(256)}, f32[256]{0:T(256)}, f32[2,256]{1,0:T(2,128)}) custom-call(s32[2]{0:T(128)} %cand_ref.1, f32[8,256]{1,0:T(8,128)} %get-tuple-element.6.total_ref, f32[8,256]{1,0:T(8,128)} %get-tuple-element.7.high_ref, f32[8,256]{1,0:T(8,128)} %get-tuple-element.8.table_ref), custom_call_target="tpu_custom_call" | custom-call | tf_op jit(solution)/shard_map/pallas_call | solution.py:537

commit v6 on v5

--- a/solution.py
+++ b/solution.py
@@ -33,87 +33,87 @@
    (4, 4, 4, 4),
    (4, 4, 4, 4),
    (2, 2, 2, 2),
-   (5, 2, 2, 5),
+   (5, 5, 2, 2),
    (5, 5, 5, 5),
-   (3, 3, 0, 3),
+   (3, 3, 3, 3),
    (0, 0, 0, 0),
-   (0, 0, 1, 1),
+   (0, 0, 0, 0),
    (1, 1, 1, 1),
    (2, 2, 1, 1),
    (3, 3, 3, 3),
-   (1, 1, 3, 3),
+   (1, 1, 1, 3),
 )
-FIRST = ((1, 0), (3, 2), (6, 0), (7, 2), (10, 2), (1, 1), (3, 3), (6, 1), (7, 3), (10, 3), (1, 2), (3, 0), (6, 3), (7, 0), (1, 3), (3, 1), (7, 1),)
+FIRST = ((1, 2), (3, 2), (6, 0), (7, 0), (10, 2), (1, 3), (3, 3), (6, 1), (7, 1), (10, 3), (1, 0), (3, 0), (6, 2), (7, 2), (1, 1), (3, 1), (6, 3), (7, 3),)
 PAIRS = (
    (1, 0, 0),
    (3, 0, 0),
    (7, 0, 0),
    (3, 7, 0),
+   (6, 7, 0),
+   (1, 7, 0),
+   (3, 6, 1),
    (1, 3, 0),
-   (1, 7, 0),
+   (1, 6, 0),
    (12, 7, 0),
+   (12, 1, 0),
    (12, 3, 0),
-   (12, 1, 0),
-   (12, 0, 0),
+   (5, 6, 0),
    (5, 1, 0),
+   (5, 7, 0),
+   (5, 12, 0),
+   (10, 1, 0),
+   (10, 7, 1),
+   (10, 5, 0),
+   (8, 5, 0),
    (8, 1, 0),
-   (8, 0, 1),
-   (5, 12, 0),
-   (5, 7, 0),
-   (5, 8, 0),
-   (6, 5, 0),
-   (6, 3, 1),
-   (6, 1, 0),
-   (10, 1, 0),
-   (10, 5, 0),
    (2, 0, 1),
-   (2, 8, 1),
    (2, 12, 0),
    (2, 7, 0),
+   (4, 12, 0),
+   (4, 7, 0),
+   (4, 6, 1),
+   (2, 8, 1),
+   (4, 8, 0),
    (11, 5, 0),
-   (11, 2, 0),
    (11, 1, 0),
    (11, 7, 1),
-   (4, 7, 0),
-   (4, 8, 0),
-   (4, 6, 1),
    (9, 1, 0),
    (9, 5, 0),
    (9, 4, 1),
 )
 ARRIVALS = (
-    ((1, 0), (3, 2), (6, 0), (7, 2), (10, 2), (1, 1), (3, 3), (6, 1), (7, 3), (10, 3), (1, 2), (3, 0), (6, 3), (7, 0), (5, 2), (12, 0), (1, 3), (3, 1), (7, 1), (12, 2),),
-    ((5, 3), (8, 2),),
-    (),
-    (),
-    (),
-    ((2, 0), (12, 3),),
-    ((5, 0), (8, 0), (12, 1),),
+    ((1, 2), (3, 2), (6, 0), (7, 0), (10, 2), (1, 3), (3, 3), (6, 1), (7, 1), (10, 3), (1, 0), (3, 0), (6, 2), (7, 2), (5, 2), (12, 0), (1, 1), (3, 1), (6, 3), (7, 3),),
+    ((5, 3), (12, 1),),
+    (),
+    (),
+    ((2, 2), (8, 0), (12, 3),),
+    ((5, 0), (12, 2),),
     ((10, 0),),
     (),
     (),
-    ((2, 1), (11, 0), (5, 1), (8, 1), (8, 3),),
-    (),
-    (),
-    (),
-    ((2, 2), (11, 2),),
-    ((4, 3), (6, 2), (9, 0),),
+    ((2, 3), (8, 1), (11, 0),),
+    ((5, 1), (9, 0),),
     ((10, 1),),
     (),
     (),
-    ((2, 3), (11, 3),),
-    ((4, 0), (9, 2),),
-    ((4, 1),),
-    (),
-    (),
-    ((11, 1),),
+    ((2, 0), (8, 2), (11, 1),),
+    ((9, 1),),
+    ((4, 0), (4, 2),),
+    (),
+    ((2, 1), (8, 3), (11, 3),),
     ((9, 3),),
-    ((4, 2),),
-    (),
-    (),
-    (),
-    (),
-    ((9, 1),),
+    ((4, 1), (4, 3),),
+    (),
+    (),
+    ((11, 2),),
+    ((9, 2),),
+    (),
+    (),
+    (),
+    (),
+    (),
+    (),
+    (),
     (),
     (),
     (),

time: 41.3 us -> 40.2 us (0.973)
  the two profiles are of different devices: /device:TPU:0 before, /device:TPU:1 now
where the time goes in v6:
time: 40.2 us; the launch traced here: 40 us
  Pallas kernels  39.4 us (98%)
  between operations  0.64 us (2%)
    pallas_call x1, Pallas kernels, per_device(): pl.pallas_call(kernel, out_shape=(jax.ShapeDtypeStruct((8, ROWS), jnp.flo...  37.9 us
    pallas_call x1, Pallas kernels, per_device(): pl.pallas_call(finisher, out_shape=(jax.ShapeDtypeStruct((ROWS,), jnp.flo...  1.42 us

profile of v6, /device:TPU:1, one launch (start us, length us, event | category | flops | bytes accessed | tf_op | source)
XLA Modules:
  0.0 40.0 jit_solution(16433675858713726889)
XLA Ops:
  0.6 37.9 %shard_map.49 = (f32[8,256]{1,0:T(8,128)}, f32[8,256]{1,0:T(8,128)}, f32[8,256]{1,0:T(8,128)}) custom-call(bf16[256,768]{1,0:T(8,128)(2,1)} %embed_ref.1), custom_call_target="tpu_custom_call" | custom-call | flops 7449083904 | bytes 10223616 | tf_op jit(solution)/shard_map/pallas_call | solution.py:502
  38.6 1.4 %shard_map.50 = (f32[256]{0:T(256)}, f32[256]{0:T(256)}, f32[2,256]{1,0:T(2,128)}) custom-call(s32[2]{0:T(128)} %cand_ref.1, f32[8,256]{1,0:T(8,128)} %get-tuple-element.6.total_ref, f32[8,256]{1,0:T(8,128)} %get-tuple-element.7.high_ref, f32[8,256]{1,0:T(8,128)} %get-tuple-element.8.table_ref), custom_call_target="tpu_custom_call" | custom-call | tf_op jit(solution)/shard_map/pallas_call | solution.py:537
